TPU v7x, 32 devices: a whole 2x2x4 slice. The times are simulated.
32 devices in a mesh: section: 4 (over y, x), dp: 8 (over z, core).
Axes of the slice: x: 2, y: 2, z: 4, core: 2. Of those that a mesh axis runs over, the one named last changes fastest.
Arguments:
- arrive: bfloat16 [4, 512, 4096], P('section', 'dp'), may hold values from -6 to 6
- entering: bfloat16 [2, 512, 4096], P(None, 'dp'), may hold values from -6 to 6
- stash: bfloat16 [4, 3, 512, 4096], P('section', None, 'dp'), may hold values from -6 to 6
- back_arrive: bfloat16 [4, 512, 4096], P('section', 'dp'), may hold values from -6 to 6
- head_grad: bfloat16 [2, 512, 4096], P(None, 'dp'), may hold values from -6 to 6
- norm_gain: float32 [4, 4096], P('section'), may hold values from 0.5 to 1.5
- router: float32 [4, 4096], P('section'), may hold values from -0.09375 to 0.09375
- w_up: bfloat16 [4, 4096, 8192], P('section', None, 'dp'), may hold values from -0.09375 to 0.09375
- w_down: bfloat16 [4, 8192, 4096], P('section', 'dp'), may hold values from -0.0625 to 0.0625
- routes: int32 [4, 3, 2, 96], P('section', None, None, 'dp'), may hold values from -1 to 63, as said below
Outputs:
- fwd_out: bfloat16 [4, 3, 512, 4096], P('section', None, 'dp')
- bwd_out: bfloat16 [4, 3, 512, 4096], P('section', None, 'dp')
- router_grad: float32 [4, 4096], P('section')
Inputs may be any that keep to these rules, and one draw needn't show every extreme that they name: `routes`: in each list, the 12 slots of each device name 1 to 12 distinct rows of that device's 64 tokens, filled slots first and -1 after them; in every list some device fills all 12 slots.
All inputs are finite; a program needn't handle non-finite values.
Results may differ from a plain program's by a relative error of at most 0.015.
Values may be sent and summed in bfloat16 or wider, within the bound.
No kernel may reach another device: no remote copies, remote signals or barrier semaphores. Data moves between devices by JAX's collectives and lax.ppermute only.
A program may use at most 128 MiB of HBM per device.

v0:
```python
import jax
import jax.numpy as jnp
from jax import lax
from jax.sharding import PartitionSpec as P

EPS = 1e-05
CORES = 2


def shift_section(block, step):
    count = lax.axis_size("section")
    route = [(i - step, i) for i in range(count) if 0 <= i - step < count]
    return lax.ppermute(block, "section", route)


def swap_core(block):
    count = lax.axis_size("dp")
    return lax.ppermute(block, "dp", [(i, i ^ 1) for i in range(count)])


def shift_chip(block, step):
    count = lax.axis_size("dp")
    return lax.ppermute(block, "dp", [(i, (i + CORES * step) % count) for i in range(count)])


def gather_rows(rows):
    chips = lax.axis_size("dp") // CORES
    count, width = rows.shape
    half = width // 2
    packed = jnp.concatenate([rows[:, :half], rows[:, half:]], axis=0)
    own_core = jnp.stack([packed] + [shift_chip(packed, j) for j in range(1, chips)], axis=0)
    other_core = swap_core(own_core)
    both = jnp.stack([own_core, other_core], axis=0)
    both = both.reshape(CORES * chips, 2, count, half).swapaxes(1, 2)
    return both.reshape(CORES * chips * count, width)


def scatter_sum(parts):
    chips = lax.axis_size("dp") // CORES
    width = parts.shape[1]
    half = width // 2
    count = parts.shape[0] // (CORES * chips)
    parts = parts.reshape(CORES, chips, count, 2, half).swapaxes(2, 3)
    parts = parts.reshape(CORES, chips, 2 * count, half)
    crossed = swap_core(parts[1].astype(jnp.bfloat16))
    summed = parts[0] + crossed.astype(jnp.float32)
    total = summed[0]
    for j in range(1, chips):
        total = total + shift_chip(summed[j].astype(jnp.bfloat16), -j).astype(jnp.float32)
    return jnp.concatenate([total[:count], total[count:]], axis=1)


def one_hot(route, size):
    return (route[:, None] == jnp.arange(size, dtype=route.dtype)[None, :]).astype(jnp.bfloat16)


def pick(activity, hot):
    return jnp.dot(hot, activity, preferred_element_type=jnp.float32)


def put(activity, hot, rows):
    taken = jnp.sum(hot.astype(jnp.float32), axis=0) > 0.5
    moved = lax.dot_general(
        hot, rows, (((0,), (0,)), ((), ())), preferred_element_type=jnp.float32
    ).astype(jnp.bfloat16)
    return jnp.where(taken[:, None], moved, activity)


def normalize(picked, gain):
    inv_rms = lax.rsqrt(jnp.mean(picked * picked, axis=-1, keepdims=True) + EPS)
    return inv_rms, (picked * inv_rms * gain).astype(jnp.bfloat16)


def gate_of(normed, router_vec):
    return jax.nn.sigmoid(
        jnp.dot(normed.astype(jnp.float32), router_vec, precision=lax.Precision.HIGHEST)
    )


def per_device(
    arrive, entering, stash, back_arrive, head_grad, norm_gain, router, w_up, w_down, routes
):
    section = lax.axis_index("section")
    last = lax.axis_size("section") - 1
    dp_count = lax.axis_size("dp")
    gain = norm_gain[0]
    router_vec = router[0]
    up_weight = w_up[0]
    down_weight = w_down[0]
    slots = routes.shape[3]
    tokens = arrive.shape[1]
    width = arrive.shape[2]
    ticks = stash.shape[1]
    contract_last = (((1,), (1,)), ((), ()))

    hot_f = [one_hot(routes[0, k, 0], tokens) for k in range(ticks)]
    hot_b = [one_hot(routes[0, k, 1], tokens) for k in range(ticks)]
    route_behind = shift_section(routes[0, :, 0], 1)
    route_ahead = shift_section(routes[0, :, 1], -1)
    route_behind = jnp.where(section == 0, -1, route_behind)
    route_ahead = jnp.where(section == last, -1, route_ahead)
    hot_behind = [one_hot(route_behind[k], tokens) for k in range(ticks)]
    hot_ahead = [one_hot(route_ahead[k], tokens) for k in range(ticks)]

    forward_in = arrive[0]
    backward_in = back_arrive[0]
    forward_rows = pick(forward_in, hot_f[0])
    backward_rows = pick(backward_in, hot_b[0]).astype(jnp.bfloat16)

    saved = jnp.stack([pick(stash[0, k], hot_b[k]) for k in range(ticks)], axis=0)
    saved_rms, saved_normed = normalize(saved, gain)

    forward_rms, forward_normed = normalize(forward_rows, gain)
    forward_all = gather_rows(forward_normed)
    saved_all = gather_rows(saved_normed.reshape(ticks * slots, width))
    saved_gate = gate_of(saved_all, router_vec).reshape(dp_count, ticks, slots)
    saved_up = jnp.dot(saved_all, up_weight, preferred_element_type=jnp.float32)
    saved_up = saved_up.reshape(dp_count, ticks, slots, -1)
    saved_all = saved_all.reshape(dp_count, ticks, slots, width)

    forward_list = []
    backward_list = []
    logit_list = []
    for k in range(ticks):
        if k + 1 < ticks:
            forward_base = shift_section(forward_in, 1)
            backward_base = shift_section(backward_in, -1)

        if k > 0:
            forward_rms, forward_normed = normalize(forward_rows, gain)
            forward_all = gather_rows(forward_normed)
        gate = gate_of(forward_normed, router_vec)
        up = jnp.dot(forward_all, up_weight, preferred_element_type=jnp.float32)
        hidden = (up * jax.nn.sigmoid(up)).astype(jnp.bfloat16)
        block = scatter_sum(jnp.dot(hidden, down_weight, preferred_element_type=jnp.float32))
        forward_new = (forward_rows + gate[:, None] * block).astype(jnp.bfloat16)
        forward_list.append(put(forward_in, hot_f[k], forward_new))

        gate_all = saved_gate[:, k].reshape(dp_count * slots, 1)
        up_b = saved_up[:, k].reshape(dp_count * slots, -1)
        upstream_all = gather_rows(backward_rows)
        grad_hidden = gate_all * lax.dot_general(
            upstream_all, down_weight, contract_last, preferred_element_type=jnp.float32
        )
        sig = jax.nn.sigmoid(up_b)
        inner = jnp.sum(grad_hidden * (up_b * sig), axis=-1, keepdims=True)
        logit = inner * (1.0 - gate_all)
        logit_list.append(logit)
        grad_up = (grad_hidden * sig * (1.0 + up_b * (1.0 - sig))).astype(jnp.bfloat16)
        grad_part = lax.dot_general(
            grad_up, up_weight, contract_last, preferred_element_type=jnp.float32
        )
        grad_normed = scatter_sum(grad_part + logit * router_vec)
        scaled_grad = grad_normed * gain
        unit = saved[k] * saved_rms[k]
        grad_rows = saved_rms[k] * (
            scaled_grad - unit * jnp.mean(scaled_grad * unit, axis=-1, keepdims=True)
        )
        backward_new = (backward_rows.astype(jnp.float32) + grad_rows).astype(jnp.bfloat16)
        backward_list.append(put(backward_in, hot_b[k], backward_new))

        if k + 1 < ticks:
            forward_moved = shift_section(forward_new, 1)
            backward_moved = shift_section(backward_new, -1)
            match_f = routes[0, k + 1, 0][:, None] == route_behind[k][None, :]
            match_f = match_f & (route_behind[k] >= 0)[None, :]
            match_b = routes[0, k + 1, 1][:, None] == route_ahead[k][None, :]
            match_b = match_b & (route_ahead[k] >= 0)[None, :]
            source_f = jnp.where(section == 0, entering[k], forward_base)
            source_b = jnp.where(section == last, head_grad[k], backward_base)
            forward_rows = jnp.where(
                jnp.any(match_f, axis=1, keepdims=True),
                jnp.dot(
                    match_f.astype(jnp.bfloat16), forward_moved, preferred_element_type=jnp.float32
                ),
                pick(source_f, hot_f[k + 1]),
            )
            backward_rows = jnp.where(
                jnp.any(match_b, axis=1, keepdims=True),
                jnp.dot(
                    match_b.astype(jnp.bfloat16), backward_moved, preferred_element_type=jnp.float32
                ),
                pick(source_b, hot_b[k + 1]),
            ).astype(jnp.bfloat16)
            forward_in = put(source_f, hot_behind[k], forward_moved)
            backward_in = put(source_b, hot_ahead[k], backward_moved)

    logits = jnp.stack(logit_list, axis=0).reshape(ticks, dp_count, slots).swapaxes(0, 1)
    router_sum = jnp.einsum(
        "dts,dtsw->w", logits, saved_all.astype(jnp.float32), precision=lax.Precision.HIGHEST
    )[None]
    chips = dp_count // CORES
    router_sum = router_sum + swap_core(router_sum)
    by_distance = jnp.concatenate(
        [router_sum] + [shift_chip(router_sum, j) for j in range(1, chips)], axis=0
    )
    chip = lax.axis_index("dp") // CORES
    total = jnp.zeros_like(router_sum)
    for j in range(chips):
        total = total + lax.dynamic_slice_in_dim(by_distance, (chip - j) % chips, 1, 0)
    scale = 1.0 / float(ticks * slots * dp_count)
    return (
        jnp.stack(forward_list, axis=0)[None],
        jnp.stack(backward_list, axis=0)[None],
        total * scale,
    )


def solution(mesh):
    in_specs = (
        P("section", "dp", None),
        P(None, "dp", None),
        P("section", None, "dp", None),
        P("section", "dp", None),
        P(None, "dp", None),
        P("section", None),
        P("section", None),
        P("section", None, "dp"),
        P("section", "dp", None),
        P("section", None, None, "dp"),
    )
    out_specs = (P("section", None, "dp", None), P("section", None, "dp", None), P("section", None))
    return jax.shard_map(
        per_device, mesh=mesh, in_specs=in_specs, out_specs=out_specs, check_vma=False
    )
```

profile of v0, /device:TPU:0, one launch (start us, length us, event | category | flops | bytes accessed | tf_op | source)
XLA Modules:
  0.0 406.0 jit_solution(8337690731028634265)
XLA Ops:
  6.6 3.1 collective-permute-start.29
  20.5 14.4 %dot_general.140 = bf16[2,2048,1024]{1,0,2:T(2,128)(2,1)} reshape(bf16[4096,1024]{0,1:T(8,128)(2,1)} %bitcast.465) | data formatting | bytes 16777216 | tf_op jit(solution)/shard_map/dot_general | solution.py:135
  35.0 21.3 %copy.143 = bf16[2,2048,1024,1,1]{2,1,0,4,3:T(8,128)(2,1)} copy(bf16[2,2048,1024,1,1]{1,0,2,4,3:T(2,128)(2,1)} %bitcast.466) | data formatting | bytes 16777216 | tf_op jit(solution)/shard_map/dot_general | solution.py:135
  59.1 4.5 %collective-permute-start.8 = (s32[3,12]{1,0:T(4,128)S(1)}, s32[3,12]{1,0:T(4,128)S(1)}, u32[]{:S(2)}, u32[]{:S(2)}) collective-permute-start(s32[3,12]{1,0:T(4,128)S(1)} %bitcast.551), channel_id=1, source_target_pairs={{0,8},{8,16},{16,24},{1,9},{9,17},{17,25},{2,10},{10,18},{18,26},{... | collective-permute-start | bytes 440 | tf_op jit(solution)/shard_map/ppermute | solution.py:13
  66.7 2.8 collective-permute-start.35
  74.0 5.9 %collective-permute-start.10 = (bf16[64,4096]{1,0:T(8,128)(2,1)}, bf16[64,4096]{1,0:T(8,128)(2,1)}, u32[]{:S(2)}, u32[]{:S(2)}) collective-permute-start(bf16[64,4096]{1,0:T(8,128)(2,1)} %bitcast.1), channel_id=1, source_target_pairs={{0,8},{8,16},{16,24},{1,9},{9,17},{17,25},{2,10},{10,18},{18,26},{... | collective-permute-start | bytes 1572872 | tf_op jit(solution)/shard_map/ppermute | solution.py:13
  84.7 3.0 pad_maximum_fusion
  87.6 2.6 reshape.400
  90.2 3.9 copy.127
  94.2 3.8 copy.124
  98.0 5.5 %dot_general.165 = bf16[8,3,12,4096]{3,0,2,1:T(8,128)(2,1)S(1)} reshape(bf16[8,36,2,2048]{3,2,0,1:T(2,128)(2,1)} %copy.127) | data formatting | bytes 4718592 | tf_op jit(solution)/shard_map/dot_general | solution.py:117
  105.1 6.0 %fusion = f32[8,3,12,1024]{3,2,1,0:T(8,128)S(1)} fusion(bf16[1,4096,1024]{2,1,0:T(8,128)(2,1)} %param.17, bf16[8,3,12,4096]{3,0,2,1:T(8,128)(2,1)S(1)} %dot_general.165), kind=kOutput, calls=%fused_computation | convolution fusion | flops 2415919104 | bytes 11927552 | tf_op jit(solution)/shard_map/dot_general | solution.py:117
  117.9 6.2 %multiply_reduce_fusion.3 = (f32[96]{0:T(128)S(1)}, f32[96,1024]{1,0:T(8,128)S(1)}) fusion(f32[96,1024]{1,0:T(8,128)S(1)} %reshape_squeeze.12, bf16[96,4096]{1,0:T(8,128)(2,1)S(1)} %bitcast.483, bf16[1,1024,4096]{2,1,0:T(8,128)(2,1)} %param.18, f32[96]{0:T(128)S(1)} %mul.408), kind=kOutput, calls=%fused_computation.134 | convolution fusion | flops 805994368 | bytes 9962240 | tf_op jit(solution)/shard_map/dot_general | solution.py:142
  124.7 6.2 %fusion.23 = f32[96,4096]{1,0:T(8,128)S(1)} fusion(bf16[1,4096,1024]{2,1,0:T(8,128)(2,1)} %param.17, f32[4096]{0:T(1024)S(1)} %bitcast.527, f32[96]{0:T(128)S(1)} %subtract_multiply_fusion.2, f32[96,1024]{1,0:T(8,128)} %copy-done.6, f32[96,1024]{1,0:T(8,128)S(1)} %get-tuple-element.111), kind=kOutput, calls=%fused_computation.21 | convolution fusion | flops 806977536 | bytes 10764672 | tf_op jit(solution)/shard_map/dot_general | solution.py:150
  141.2 6.5 %collective-permute-done.39 = bf16[24,2048]{1,0:T(8,128)(2,1)S(1)} collective-permute-done((bf16[24,2048]{1,0:T(8,128)(2,1)S(1)}, bf16[24,2048]{1,0:T(8,128)(2,1)S(1)}, u32[]{:S(2)}, u32[]{:S(2)}) %collective-permute-start.39) | collective-permute-done | bytes 98336 | tf_op jit(solution)/shard_map/ppermute | solution.py:23
  151.0 4.9 %collective-permute-done.42 = bf16[12,4096]{1,0:T(8,128)(2,1)S(1)} collective-permute-done((bf16[12,4096]{1,0:T(8,128)(2,1)S(1)}, bf16[12,4096]{1,0:T(8,128)(2,1)S(1)}, u32[]{:S(2)}, u32[]{:S(2)}) %collective-permute-start.42) | collective-permute-done | bytes 98336 | tf_op jit(solution)/shard_map/ppermute | solution.py:13
  158.7 3.2 collective-permute-start.46
  163.7 2.7 collective-permute-done.45
  174.2 6.2 %multiply_reduce_fusion.2 = (f32[96]{0:T(128)S(1)}, f32[96,1024]{1,0:T(8,128)S(1)}) fusion(f32[96,1024]{1,0:T(8,128)S(1)} %reshape_squeeze.13, bf16[96,4096]{1,0:T(8,128)(2,1)S(1)} %bitcast.484, bf16[1,1024,4096]{2,1,0:T(8,128)(2,1)} %param.18, f32[96]{0:T(128)S(1)} %mul.428), kind=kOutput, calls=%fused_computation.131 | convolution fusion | flops 805994368 | bytes 9962240 | tf_op jit(solution)/shard_map/dot_general | solution.py:142
  180.9 6.1 %fusion.26 = f32[96,4096]{1,0:T(8,128)S(1)} fusion(bf16[1,4096,1024]{2,1,0:T(8,128)(2,1)} %param.17, f32[96]{0:T(128)S(1)} %subtract_multiply_fusion.1, f32[4096]{0:T(1024)S(1)} %bitcast.528, f32[96,1024]{1,0:T(8,128)S(1)} %reshape_squeeze.13, f32[96,1024]{1,0:T(8,128)S(1)} %get-tuple-element.113), kind=kOutput, calls=%fused_computation.22 | convolution fusion | flops 806977536 | bytes 10764672 | tf_op jit(solution)/shard_map/dot_general | solution.py:150
  196.8 3.6 collective-permute-start.49
  201.0 11.1 %collective-permute-done.53 = bf16[64,4096]{1,0:T(8,128)(2,1)} collective-permute-done((bf16[64,4096]{1,0:T(8,128)(2,1)S(1)}, bf16[64,4096]{1,0:T(8,128)(2,1)}, u32[]{:S(2)}, u32[]{:S(2)}) %collective-permute-start.53) | collective-permute-done | bytes 524320 | tf_op jit(solution)/shard_map/ppermute | solution.py:13
  222.0 4.9 %collective-permute-done.52 = bf16[12,4096]{1,0:T(8,128)(2,1)S(1)} collective-permute-done((bf16[12,4096]{1,0:T(8,128)(2,1)S(1)}, bf16[12,4096]{1,0:T(8,128)(2,1)S(1)}, u32[]{:S(2)}, u32[]{:S(2)}) %collective-permute-start.52) | collective-permute-done | bytes 98336 | tf_op jit(solution)/shard_map/ppermute | solution.py:13
  234.6 3.0 collective-permute-done.55
  239.7 4.9 %multiply_convert_fusion.6 = bf16[96,1024]{1,0:T(8,128)(2,1)S(1)} fusion(bf16[96,4096]{1,0:T(8,128)(2,1)S(1)} %bitcast.471, bf16[1,4096,1024]{2,1,0:T(8,128)(2,1)} %param.17), kind=kOutput, calls=%fused_computation.139 | convolution fusion | flops 805797888 | bytes 9371648 | tf_op jit(solution)/shard_map/dot_general | solution.py:133
  244.7 6.2 %convolution_bitcast_fusion.3 = f32[2,4,2,12,2048]{4,3,2,1,0:T(8,128)S(1)} fusion(bf16[2,2048,1024,1,1]{2,1,0,4,3:T(8,128)(2,1)} %copy.143, bf16[2,4,12,1024,1]{3,2,1,0,4:T(8,128)(2,1)S(1)} %reshape.382), kind=kOutput, calls=%fused_computation.60 | convolution fusion | flops 805306368 | bytes 10158080 | tf_op jit(solution)/shard_map/dot_general | solution.py:135
  256.3 6.4 %multiply_reduce_fusion.1 = (f32[96]{0:T(128)S(1)}, f32[96,1024]{1,0:T(8,128)S(1)}) fusion(f32[96,1024]{1,0:T(8,128)S(1)} %copy-done.5, bf16[96,4096]{1,0:T(8,128)(2,1)S(1)} %bitcast.485, bf16[1,1024,4096]{2,1,0:T(8,128)(2,1)} %param.18, f32[96]{0:T(128)S(1)} %copy-done.97), kind=kOutput, calls=%fused_computation.128 | convolution fusion | flops 805994368 | bytes 9962240 | tf_op jit(solution)/shard_map/dot_general | solution.py:142
  270.8 6.1 %fusion.20 = f32[96,4096]{1,0:T(8,128)S(1)} fusion(bf16[1,4096,1024]{2,1,0:T(8,128)(2,1)} %param.17, f32[96]{0:T(128)S(1)} %subtract_multiply_fusion, f32[4096]{0:T(1024)} %bitcast.526, f32[96,1024]{1,0:T(8,128)S(1)} %copy-done.5, f32[96,1024]{1,0:T(8,128)S(1)} %get-tuple-element.117), kind=kOutput, calls=%fused_computation.20 | convolution fusion | flops 806977536 | bytes 10764672 | tf_op jit(solution)/shard_map/dot_general | solution.py:150
  286.8 2.6 collective-permute-start.59
  290.1 5.0 %collective-permute-done.6 = bf16[24,2048]{1,0:T(8,128)(2,1)S(1)} collective-permute-done((bf16[24,2048]{1,0:T(8,128)(2,1)S(1)}, bf16[24,2048]{1,0:T(8,128)(2,1)S(1)}, u32[]{:S(2)}, u32[]{:S(2)}) %collective-permute-start.6) | collective-permute-done | bytes 98336 | tf_op jit(solution)/shard_map/ppermute | solution.py:23
  295.3 4.2 %collective-permute-start.9 = (bf16[12,4096]{1,0:T(8,128)(2,1)S(1)}, bf16[12,4096]{1,0:T(8,128)(2,1)S(1)}, u32[]{:S(2)}, u32[]{:S(2)}) collective-permute-start(bf16[12,4096]{1,0:T(8,128)(2,1)S(1)} %fusion.86), channel_id=1, source_target_pairs={{0,8},{8,16},{16,24},{1,9},{9,17},{17,25},{2,10},{10,18},{18,26},{... | collective-permute-start | bytes 294920 | tf_op jit(solution)/shard_map/ppermute | solution.py:13
  299.5 3.4 collective-permute-done.60
  304.2 3.5 collective-permute-start.11
  309.7 3.2 collective-permute-start.13
  313.0 3.0 collective-permute-done.12
  320.2 4.9 %multiply_convert_fusion.5 = bf16[96,1024]{1,0:T(8,128)(2,1)S(1)} fusion(bf16[96,4096]{1,0:T(8,128)(2,1)S(1)} %bitcast.472, bf16[1,4096,1024]{2,1,0:T(8,128)(2,1)} %param.17), kind=kOutput, calls=%fused_computation.138 | convolution fusion | flops 805797888 | bytes 9371648 | tf_op jit(solution)/shard_map/dot_general | solution.py:133
  325.2 6.2 %convolution_bitcast_fusion.2 = f32[2,4,2,12,2048]{4,3,2,1,0:T(8,128)S(1)} fusion(bf16[2,2048,1024,1,1]{2,1,0,4,3:T(8,128)(2,1)} %copy.143, bf16[2,4,12,1024,1]{3,2,1,0,4:T(8,128)(2,1)S(1)} %reshape.386), kind=kOutput, calls=%fused_computation.59 | convolution fusion | flops 805306368 | bytes 10158080 | tf_op jit(solution)/shard_map/dot_general | solution.py:135
  334.6 4.7 %collective-permute-start.16 = (bf16[24,2048]{1,0:T(8,128)(2,1)S(1)}, bf16[24,2048]{1,0:T(8,128)(2,1)S(1)}, u32[]{:S(2)}, u32[]{:S(2)}) collective-permute-start(bf16[24,2048]{1,0:T(8,128)(2,1)S(1)} %get-tuple-element.45), channel_id=1, source_target_pairs={{0,6},{1,7},{2,0},{3,1},{4,2},{5,3},{6,4},{7,5},{8,14},{9,15},{10,... | collective-permute-start | bytes 294920 | tf_op jit(solution)/shard_map/ppermute | solution.py:23
  340.0 5.5 %collective-permute-start.20 = (bf16[64,4096]{1,0:T(8,128)(2,1)S(1)}, bf16[64,4096]{1,0:T(8,128)(2,1)S(1)}, u32[]{:S(2)}, u32[]{:S(2)}) collective-permute-start(bf16[64,4096]{1,0:T(8,128)(2,1)S(1)} %fusion.31), channel_id=1, source_target_pairs={{0,8},{8,16},{16,24},{1,9},{9,17},{17,25},{2,10},{10,18},{18,26},{... | collective-permute-start | bytes 1572872 | tf_op jit(solution)/shard_map/ppermute | solution.py:13
  345.5 3.5 collective-permute-done.17
  349.2 5.4 %collective-permute-start.19 = (bf16[12,4096]{1,0:T(8,128)(2,1)S(1)}, bf16[12,4096]{1,0:T(8,128)(2,1)S(1)}, u32[]{:S(2)}, u32[]{:S(2)}) collective-permute-start(bf16[12,4096]{1,0:T(8,128)(2,1)S(1)} %fusion.88), channel_id=1, source_target_pairs={{0,8},{8,16},{16,24},{1,9},{9,17},{17,25},{2,10},{10,18},{18,26},{... | collective-permute-start | bytes 294920 | tf_op jit(solution)/shard_map/ppermute | solution.py:13
  354.6 3.2 collective-permute-done.20
  359.7 2.6 collective-permute-start.21
  367.1 3.0 collective-permute-done.22
  375.1 4.9 %multiply_convert_fusion.4 = bf16[96,1024]{1,0:T(8,128)(2,1)S(1)} fusion(bf16[96,4096]{1,0:T(8,128)(2,1)S(1)} %bitcast.473, bf16[1,4096,1024]{2,1,0:T(8,128)(2,1)} %param.17), kind=kOutput, calls=%fused_computation.137 | convolution fusion | flops 805797888 | bytes 9371648 | tf_op jit(solution)/shard_map/dot_general | solution.py:133
  380.0 6.2 %convolution_bitcast_fusion.1 = f32[2,4,2,12,2048]{4,3,2,1,0:T(8,128)S(1)} fusion(bf16[2,2048,1024,1,1]{2,1,0,4,3:T(8,128)(2,1)} %copy.143, bf16[2,4,12,1024,1]{3,2,1,0,4:T(8,128)(2,1)S(1)} %reshape.390), kind=kOutput, calls=%fused_computation.58 | convolution fusion | flops 805306368 | bytes 10158080 | tf_op jit(solution)/shard_map/dot_general | solution.py:135
  390.6 2.9 collective-permute-start.26
  396.7 6.8 %collective-permute-done.27 = bf16[24,2048]{1,0:T(8,128)(2,1)S(1)} collective-permute-done((bf16[24,2048]{1,0:T(8,128)(2,1)S(1)}, bf16[24,2048]{1,0:T(8,128)(2,1)S(1)}, u32[]{:S(2)}, u32[]{:S(2)}) %collective-permute-start.27) | collective-permute-done | bytes 98336 | tf_op jit(solution)/shard_map/ppermute | solution.py:23
  (576 shorter events, 152.5 us)
Async XLA Ops:
  6.6 60.1 %collective-permute-start.29 = (bf16[72,2048]{1,0:T(8,128)(2,1)S(1)}, bf16[72,2048]{1,0:T(8,128)(2,1)S(1)}, u32[]{:S(2)}, u32[]{:S(2)}) collective-permute-start(bf16[72,2048]{1,0:T(8,128)(2,1)S(1)} %pad_maximum_fusion.15), channel_id=1, source_target_pairs={{0,2},{1,3},{2,4},{3,5},{4,6},{5,7},{6,0},{7,1},{8,10},{9,11},{10,... | collective-permute-start | bytes 884744 | tf_op jit(solution)/shard_map/ppermute | solution.py:23
  9.6 59.9 %collective-permute-start.30 = (bf16[72,2048]{1,0:T(8,128)(2,1)S(1)}, bf16[72,2048]{1,0:T(8,128)(2,1)S(1)}, u32[]{:S(2)}, u32[]{:S(2)}) collective-permute-start(bf16[72,2048]{1,0:T(8,128)(2,1)S(1)} %pad_maximum_fusion.15), channel_id=1, source_target_pairs={{0,4},{1,5},{2,6},{3,7},{4,0},{5,1},{6,2},{7,3},{8,12},{9,13},{10,... | collective-permute-start | bytes 884744 | tf_op jit(solution)/shard_map/ppermute | solution.py:23
  12.2 58.6 %collective-permute-start.31 = (bf16[72,2048]{1,0:T(8,128)(2,1)S(1)}, bf16[72,2048]{1,0:T(8,128)(2,1)S(1)}, u32[]{:S(2)}, u32[]{:S(2)}) collective-permute-start(bf16[72,2048]{1,0:T(8,128)(2,1)S(1)} %pad_maximum_fusion.15), channel_id=1, source_target_pairs={{0,6},{1,7},{2,0},{3,1},{4,2},{5,3},{6,4},{7,5},{8,14},{9,15},{10,... | collective-permute-start | bytes 884744 | tf_op jit(solution)/shard_map/ppermute | solution.py:23
  14.9 59.1 %collective-permute-start.33 = (bf16[24,2048]{1,0:T(8,128)(2,1)S(1)}, bf16[24,2048]{1,0:T(8,128)(2,1)S(1)}, u32[]{:S(2)}, u32[]{:S(2)}) collective-permute-start(bf16[24,2048]{1,0:T(8,128)(2,1)S(1)} %pad_maximum_fusion.19), channel_id=1, source_target_pairs={{0,2},{1,3},{2,4},{3,5},{4,6},{5,7},{6,0},{7,1},{8,10},{9,11},{10,... | collective-permute-start | bytes 294920 | tf_op jit(solution)/shard_map/ppermute | solution.py:23
  15.7 43.4 %collective-permute-start.41 = (s32[3,12]{1,0:T(4,128)S(1)}, s32[3,12]{1,0:T(4,128)S(1)}, u32[]{:S(2)}, u32[]{:S(2)}) collective-permute-start(s32[3,12]{1,0:T(4,128)S(1)} %bitcast.550), channel_id=1, source_target_pairs={{8,0},{16,8},{24,16},{9,1},{17,9},{25,17},{10,2},{18,10},{26,18},{... | collective-permute-start | bytes 440 | tf_op jit(solution)/shard_map/ppermute | solution.py:13
  64.9 14.9 %collective-permute-start.34 = (bf16[24,2048]{1,0:T(8,128)(2,1)S(1)}, bf16[24,2048]{1,0:T(8,128)(2,1)S(1)}, u32[]{:S(2)}, u32[]{:S(2)}) collective-permute-start(bf16[24,2048]{1,0:T(8,128)(2,1)S(1)} %pad_maximum_fusion.19), channel_id=1, source_target_pairs={{0,4},{1,5},{2,6},{3,7},{4,0},{5,1},{6,2},{7,3},{8,12},{9,13},{10,... | collective-permute-start | bytes 294920 | tf_op jit(solution)/shard_map/ppermute | solution.py:23
  66.7 13.2 %collective-permute-start.35 = (bf16[24,2048]{1,0:T(8,128)(2,1)S(1)}, bf16[24,2048]{1,0:T(8,128)(2,1)S(1)}, u32[]{:S(2)}, u32[]{:S(2)}) collective-permute-start(bf16[24,2048]{1,0:T(8,128)(2,1)S(1)} %pad_maximum_fusion.19), channel_id=1, source_target_pairs={{0,6},{1,7},{2,0},{3,1},{4,2},{5,3},{6,4},{7,5},{8,14},{9,15},{10,... | collective-permute-start | bytes 294920 | tf_op jit(solution)/shard_map/ppermute | solution.py:23
  69.5 80.2 %collective-permute-start.43 = (bf16[64,4096]{1,0:T(8,128)(2,1)}, bf16[64,4096]{1,0:T(8,128)(2,1)}, u32[]{:S(2)}, u32[]{:S(2)}) collective-permute-start(bf16[64,4096]{1,0:T(8,128)(2,1)} %bitcast.74), channel_id=1, source_target_pairs={{8,0},{16,8},{24,16},{9,1},{17,9},{25,17},{10,2},{18,10},{26,18},{... | collective-permute-start | bytes 1572872 | tf_op jit(solution)/shard_map/ppermute | solution.py:13
  72.0 12.7 %collective-permute-start.32 = (bf16[4,72,2048]{2,1,0:T(8,128)(2,1)}, bf16[4,72,2048]{2,1,0:T(8,128)(2,1)}, u32[]{:S(2)}, u32[]{:S(2)}) collective-permute-start(bf16[4,72,2048]{2,1,0:T(8,128)(2,1)} %get-tuple-element.22), channel_id=1, source_target_pairs={{0,1},{1,0},{2,3},{3,2},{4,5},{5,4},{6,7},{7,6},{8,9},{9,8},{10,11... | collective-permute-start | bytes 3538952 | tf_op jit(solution)/shard_map/ppermute | solution.py:18
  74.0 93.3 %collective-permute-start.10 = (bf16[64,4096]{1,0:T(8,128)(2,1)}, bf16[64,4096]{1,0:T(8,128)(2,1)}, u32[]{:S(2)}, u32[]{:S(2)}) collective-permute-start(bf16[64,4096]{1,0:T(8,128)(2,1)} %bitcast.1), channel_id=1, source_target_pairs={{0,8},{8,16},{16,24},{1,9},{9,17},{17,25},{2,10},{10,18},{18,26},{... | collective-permute-start | bytes 1572872 | tf_op jit(solution)/shard_map/ppermute | solution.py:13
  137.4 10.3 %collective-permute-start.39 = (bf16[24,2048]{1,0:T(8,128)(2,1)S(1)}, bf16[24,2048]{1,0:T(8,128)(2,1)S(1)}, u32[]{:S(2)}, u32[]{:S(2)}) collective-permute-start(bf16[24,2048]{1,0:T(8,128)(2,1)S(1)} %get-tuple-element.37), channel_id=1, source_target_pairs={{0,4},{1,5},{2,6},{3,7},{4,0},{5,1},{6,2},{7,3},{8,12},{9,13},{10,... | collective-permute-start | bytes 294920 | tf_op jit(solution)/shard_map/ppermute | solution.py:23
  138.3 9.4 %collective-permute-start.40 = (bf16[24,2048]{1,0:T(8,128)(2,1)S(1)}, bf16[24,2048]{1,0:T(8,128)(2,1)S(1)}, u32[]{:S(2)}, u32[]{:S(2)}) collective-permute-start(bf16[24,2048]{1,0:T(8,128)(2,1)S(1)} %get-tuple-element.36), channel_id=1, source_target_pairs={{0,2},{1,3},{2,4},{3,5},{4,6},{5,7},{6,0},{7,1},{8,10},{9,11},{10,... | collective-permute-start | bytes 294920 | tf_op jit(solution)/shard_map/ppermute | solution.py:23
  148.2 7.7 %collective-permute-start.42 = (bf16[12,4096]{1,0:T(8,128)(2,1)S(1)}, bf16[12,4096]{1,0:T(8,128)(2,1)S(1)}, u32[]{:S(2)}, u32[]{:S(2)}) collective-permute-start(bf16[12,4096]{1,0:T(8,128)(2,1)S(1)} %add_convert_fusion.2), channel_id=1, source_target_pairs={{8,0},{16,8},{24,16},{9,1},{17,9},{25,17},{10,2},{18,10},{26,18},{... | collective-permute-start | bytes 294920 | tf_op jit(solution)/shard_map/ppermute | solution.py:13
  156.2 7.5 %collective-permute-start.44 = (bf16[24,2048]{1,0:T(8,128)(2,1)S(1)}, bf16[24,2048]{1,0:T(8,128)(2,1)S(1)}, u32[]{:S(2)}, u32[]{:S(2)}) collective-permute-start(bf16[24,2048]{1,0:T(8,128)(2,1)S(1)} %pad_maximum_fusion.20), channel_id=1, source_target_pairs={{0,2},{1,3},{2,4},{3,5},{4,6},{5,7},{6,0},{7,1},{8,10},{9,11},{10,... | collective-permute-start | bytes 294920 | tf_op jit(solution)/shard_map/ppermute | solution.py:23
  156.7 9.8 %collective-permute-start.45 = (bf16[24,2048]{1,0:T(8,128)(2,1)S(1)}, bf16[24,2048]{1,0:T(8,128)(2,1)S(1)}, u32[]{:S(2)}, u32[]{:S(2)}) collective-permute-start(bf16[24,2048]{1,0:T(8,128)(2,1)S(1)} %pad_maximum_fusion.20), channel_id=1, source_target_pairs={{0,4},{1,5},{2,6},{3,7},{4,0},{5,1},{6,2},{7,3},{8,12},{9,13},{10,... | collective-permute-start | bytes 294920 | tf_op jit(solution)/shard_map/ppermute | solution.py:23
  158.7 7.8 %collective-permute-start.46 = (bf16[24,2048]{1,0:T(8,128)(2,1)S(1)}, bf16[24,2048]{1,0:T(8,128)(2,1)S(1)}, u32[]{:S(2)}, u32[]{:S(2)}) collective-permute-start(bf16[24,2048]{1,0:T(8,128)(2,1)S(1)} %pad_maximum_fusion.20), channel_id=1, source_target_pairs={{0,6},{1,7},{2,0},{3,1},{4,2},{5,3},{6,4},{7,5},{8,14},{9,15},{10,... | collective-permute-start | bytes 294920 | tf_op jit(solution)/shard_map/ppermute | solution.py:23
  194.2 18.0 %collective-permute-start.53 = (bf16[64,4096]{1,0:T(8,128)(2,1)S(1)}, bf16[64,4096]{1,0:T(8,128)(2,1)}, u32[]{:S(2)}, u32[]{:S(2)}) collective-permute-start(bf16[64,4096]{1,0:T(8,128)(2,1)S(1)} %fusion.35), channel_id=1, source_target_pairs={{8,0},{16,8},{24,16},{9,1},{17,9},{25,17},{10,2},{18,10},{26,18},{... | collective-permute-start | bytes 1572872 | tf_op jit(solution)/shard_map/ppermute | solution.py:13
  196.8 16.7 %collective-permute-start.49 = (bf16[24,2048]{1,0:T(8,128)(2,1)S(1)}, bf16[24,2048]{1,0:T(8,128)(2,1)S(1)}, u32[]{:S(2)}, u32[]{:S(2)}) collective-permute-start(bf16[24,2048]{1,0:T(8,128)(2,1)S(1)} %get-tuple-element.30), channel_id=1, source_target_pairs={{0,6},{1,7},{2,0},{3,1},{4,2},{5,3},{6,4},{7,5},{8,14},{9,15},{10,... | collective-permute-start | bytes 294920 | tf_op jit(solution)/shard_map/ppermute | solution.py:23
  200.4 13.1 %collective-permute-start.50 = (bf16[24,2048]{1,0:T(8,128)(2,1)S(1)}, bf16[24,2048]{1,0:T(8,128)(2,1)S(1)}, u32[]{:S(2)}, u32[]{:S(2)}) collective-permute-start(bf16[24,2048]{1,0:T(8,128)(2,1)S(1)} %get-tuple-element.32), channel_id=1, source_target_pairs={{0,4},{1,5},{2,6},{3,7},{4,0},{5,1},{6,2},{7,3},{8,12},{9,13},{10,... | collective-permute-start | bytes 294920 | tf_op jit(solution)/shard_map/ppermute | solution.py:23
  200.4 13.1 %collective-permute-start.51 = (bf16[24,2048]{1,0:T(8,128)(2,1)S(1)}, bf16[24,2048]{1,0:T(8,128)(2,1)S(1)}, u32[]{:S(2)}, u32[]{:S(2)}) collective-permute-start(bf16[24,2048]{1,0:T(8,128)(2,1)S(1)} %get-tuple-element.31), channel_id=1, source_target_pairs={{0,2},{1,3},{2,4},{3,5},{4,6},{5,7},{6,0},{7,1},{8,10},{9,11},{10,... | collective-permute-start | bytes 294920 | tf_op jit(solution)/shard_map/ppermute | solution.py:23
  214.1 16.1 %collective-permute-start = (bf16[24,2048]{1,0:T(8,128)(2,1)S(1)}, bf16[24,2048]{1,0:T(8,128)(2,1)S(1)}, u32[]{:S(2)}, u32[]{:S(2)}) collective-permute-start(bf16[24,2048]{1,0:T(8,128)(2,1)S(1)} %pad_maximum_fusion.16), channel_id=1, source_target_pairs={{0,2},{1,3},{2,4},{3,5},{4,6},{5,7},{6,0},{7,1},{8,10},{9,11},{10,... | collective-permute-start | bytes 294920 | tf_op jit(solution)/shard_map/ppermute | solution.py:23
  216.0 16.5 %collective-permute-start.1 = (bf16[24,2048]{1,0:T(8,128)(2,1)S(1)}, bf16[24,2048]{1,0:T(8,128)(2,1)S(1)}, u32[]{:S(2)}, u32[]{:S(2)}) collective-permute-start(bf16[24,2048]{1,0:T(8,128)(2,1)S(1)} %pad_maximum_fusion.16), channel_id=1, source_target_pairs={{0,4},{1,5},{2,6},{3,7},{4,0},{5,1},{6,2},{7,3},{8,12},{9,13},{10,... | collective-permute-start | bytes 294920 | tf_op jit(solution)/shard_map/ppermute | solution.py:23
  218.2 14.3 %collective-permute-start.2 = (bf16[24,2048]{1,0:T(8,128)(2,1)S(1)}, bf16[24,2048]{1,0:T(8,128)(2,1)S(1)}, u32[]{:S(2)}, u32[]{:S(2)}) collective-permute-start(bf16[24,2048]{1,0:T(8,128)(2,1)S(1)} %pad_maximum_fusion.16), channel_id=1, source_target_pairs={{0,6},{1,7},{2,0},{3,1},{4,2},{5,3},{6,4},{7,5},{8,14},{9,15},{10,... | collective-permute-start | bytes 294920 | tf_op jit(solution)/shard_map/ppermute | solution.py:23
  219.4 7.5 %collective-permute-start.52 = (bf16[12,4096]{1,0:T(8,128)(2,1)S(1)}, bf16[12,4096]{1,0:T(8,128)(2,1)S(1)}, u32[]{:S(2)}, u32[]{:S(2)}) collective-permute-start(bf16[12,4096]{1,0:T(8,128)(2,1)S(1)} %get-tuple-element.89), channel_id=1, source_target_pairs={{8,0},{16,8},{24,16},{9,1},{17,9},{25,17},{10,2},{18,10},{26,18},{... | collective-permute-start | bytes 294920 | tf_op jit(solution)/shard_map/ppermute | solution.py:13
  229.5 8.0 %collective-permute-start.55 = (bf16[24,2048]{1,0:T(8,128)(2,1)S(1)}, bf16[24,2048]{1,0:T(8,128)(2,1)S(1)}, u32[]{:S(2)}, u32[]{:S(2)}) collective-permute-start(bf16[24,2048]{1,0:T(8,128)(2,1)S(1)} %pad_maximum_fusion.21), channel_id=1, source_target_pairs={{0,4},{1,5},{2,6},{3,7},{4,0},{5,1},{6,2},{7,3},{8,12},{9,13},{10,... | collective-permute-start | bytes 294920 | tf_op jit(solution)/shard_map/ppermute | solution.py:23
  237.6 16.6 %collective-permute-start.57 = (bf16[4,24,2048]{2,1,0:T(8,128)(2,1)S(1)}, bf16[4,24,2048]{2,1,0:T(8,128)(2,1)S(1)}, u32[]{:S(2)}, u32[]{:S(2)}) collective-permute-start(bf16[4,24,2048]{2,1,0:T(8,128)(2,1)S(1)} %get-tuple-element.29), channel_id=1, source_target_pairs={{0,1},{1,0},{2,3},{3,2},{4,5},{5,4},{6,7},{7,6},{8,9},{9,8},{10,11... | collective-permute-start | bytes 1179656 | tf_op jit(solution)/shard_map/ppermute | solution.py:18
  253.7 27.0 %collective-permute-start.4 = (bf16[4,24,2048]{2,1,0:T(8,128)(2,1)}, bf16[4,24,2048]{2,1,0:T(8,128)(2,1)}, u32[]{:S(2)}, u32[]{:S(2)}) collective-permute-start(bf16[4,24,2048]{2,1,0:T(8,128)(2,1)} %copy.107), channel_id=1, source_target_pairs={{0,1},{1,0},{2,3},{3,2},{4,5},{5,4},{6,7},{7,6},{8,9},{9,8},{10,11... | collective-permute-start | bytes 1179656 | tf_op jit(solution)/shard_map/ppermute | solution.py:18
  266.8 13.0 %collective-permute-start.63 = (f32[1,4096]{1,0:T(1,128)}, f32[1,4096]{1,0:T(1,128)}, u32[]{:S(2)}, u32[]{:S(2)}) collective-permute-start(f32[1,4096]{1,0:T(1,128)} %add.271), channel_id=1, source_target_pairs={{0,2},{1,3},{2,4},{3,5},{4,6},{5,7},{6,0},{7,1},{8,10},{9,11},{10,... | collective-permute-start | bytes 49160 | tf_op jit(solution)/shard_map/ppermute | solution.py:23
  268.4 11.4 %collective-permute-start.64 = (f32[1,4096]{1,0:T(1,128)}, f32[1,4096]{1,0:T(1,128)}, u32[]{:S(2)}, u32[]{:S(2)}) collective-permute-start(f32[1,4096]{1,0:T(1,128)} %add.271), channel_id=1, source_target_pairs={{0,4},{1,5},{2,6},{3,7},{4,0},{5,1},{6,2},{7,3},{8,12},{9,13},{10,... | collective-permute-start | bytes 49160 | tf_op jit(solution)/shard_map/ppermute | solution.py:23
  270.0 9.9 %collective-permute-start.65 = (f32[1,4096]{1,0:T(1,128)}, f32[1,4096]{1,0:T(1,128)}, u32[]{:S(2)}, u32[]{:S(2)}) collective-permute-start(f32[1,4096]{1,0:T(1,128)} %add.271), channel_id=1, source_target_pairs={{0,6},{1,7},{2,0},{3,1},{4,2},{5,3},{6,4},{7,5},{8,14},{9,15},{10,... | collective-permute-start | bytes 49160 | tf_op jit(solution)/shard_map/ppermute | solution.py:23
  282.2 7.7 %collective-permute-start.5 = (bf16[24,2048]{1,0:T(8,128)(2,1)S(1)}, bf16[24,2048]{1,0:T(8,128)(2,1)S(1)}, u32[]{:S(2)}, u32[]{:S(2)}) collective-permute-start(bf16[24,2048]{1,0:T(8,128)(2,1)S(1)} %get-tuple-element.50), channel_id=1, source_target_pairs={{0,6},{1,7},{2,0},{3,1},{4,2},{5,3},{6,4},{7,5},{8,14},{9,15},{10,... | collective-permute-start | bytes 294920 | tf_op jit(solution)/shard_map/ppermute | solution.py:23
  284.3 10.7 %collective-permute-start.6 = (bf16[24,2048]{1,0:T(8,128)(2,1)S(1)}, bf16[24,2048]{1,0:T(8,128)(2,1)S(1)}, u32[]{:S(2)}, u32[]{:S(2)}) collective-permute-start(bf16[24,2048]{1,0:T(8,128)(2,1)S(1)} %get-tuple-element.52), channel_id=1, source_target_pairs={{0,4},{1,5},{2,6},{3,7},{4,0},{5,1},{6,2},{7,3},{8,12},{9,13},{10,... | collective-permute-start | bytes 294920 | tf_op jit(solution)/shard_map/ppermute | solution.py:23
  285.0 10.1 %collective-permute-start.7 = (bf16[24,2048]{1,0:T(8,128)(2,1)S(1)}, bf16[24,2048]{1,0:T(8,128)(2,1)S(1)}, u32[]{:S(2)}, u32[]{:S(2)}) collective-permute-start(bf16[24,2048]{1,0:T(8,128)(2,1)S(1)} %get-tuple-element.51), channel_id=1, source_target_pairs={{0,2},{1,3},{2,4},{3,5},{4,6},{5,7},{6,0},{7,1},{8,10},{9,11},{10,... | collective-permute-start | bytes 294920 | tf_op jit(solution)/shard_map/ppermute | solution.py:23
  286.8 12.7 %collective-permute-start.59 = (bf16[24,2048]{1,0:T(8,128)(2,1)S(1)}, bf16[24,2048]{1,0:T(8,128)(2,1)S(1)}, u32[]{:S(2)}, u32[]{:S(2)}) collective-permute-start(bf16[24,2048]{1,0:T(8,128)(2,1)S(1)} %get-tuple-element.25), channel_id=1, source_target_pairs={{0,6},{1,7},{2,0},{3,1},{4,2},{5,3},{6,4},{7,5},{8,14},{9,15},{10,... | collective-permute-start | bytes 294920 | tf_op jit(solution)/shard_map/ppermute | solution.py:23
  289.4 13.5 %collective-permute-start.60 = (bf16[24,2048]{1,0:T(8,128)(2,1)S(1)}, bf16[24,2048]{1,0:T(8,128)(2,1)S(1)}, u32[]{:S(2)}, u32[]{:S(2)}) collective-permute-start(bf16[24,2048]{1,0:T(8,128)(2,1)S(1)} %get-tuple-element.27), channel_id=1, source_target_pairs={{0,4},{1,5},{2,6},{3,7},{4,0},{5,1},{6,2},{7,3},{8,12},{9,13},{10,... | collective-permute-start | bytes 294920 | tf_op jit(solution)/shard_map/ppermute | solution.py:23
  289.9 13.0 %collective-permute-start.61 = (bf16[24,2048]{1,0:T(8,128)(2,1)S(1)}, bf16[24,2048]{1,0:T(8,128)(2,1)S(1)}, u32[]{:S(2)}, u32[]{:S(2)}) collective-permute-start(bf16[24,2048]{1,0:T(8,128)(2,1)S(1)} %get-tuple-element.26), channel_id=1, source_target_pairs={{0,2},{1,3},{2,4},{3,5},{4,6},{5,7},{6,0},{7,1},{8,10},{9,11},{10,... | collective-permute-start | bytes 294920 | tf_op jit(solution)/shard_map/ppermute | solution.py:23
  295.3 7.7 %collective-permute-start.9 = (bf16[12,4096]{1,0:T(8,128)(2,1)S(1)}, bf16[12,4096]{1,0:T(8,128)(2,1)S(1)}, u32[]{:S(2)}, u32[]{:S(2)}) collective-permute-start(bf16[12,4096]{1,0:T(8,128)(2,1)S(1)} %fusion.86), channel_id=1, source_target_pairs={{0,8},{8,16},{16,24},{1,9},{9,17},{17,25},{2,10},{10,18},{18,26},{... | collective-permute-start | bytes 294920 | tf_op jit(solution)/shard_map/ppermute | solution.py:13
  304.2 8.7 %collective-permute-start.11 = (bf16[24,2048]{1,0:T(8,128)(2,1)S(1)}, bf16[24,2048]{1,0:T(8,128)(2,1)S(1)}, u32[]{:S(2)}, u32[]{:S(2)}) collective-permute-start(bf16[24,2048]{1,0:T(8,128)(2,1)S(1)} %pad_maximum_fusion.17), channel_id=1, source_target_pairs={{0,2},{1,3},{2,4},{3,5},{4,6},{5,7},{6,0},{7,1},{8,10},{9,11},{10,... | collective-permute-start | bytes 294920 | tf_op jit(solution)/shard_map/ppermute | solution.py:23
  307.7 8.3 %collective-permute-start.12 = (bf16[24,2048]{1,0:T(8,128)(2,1)S(1)}, bf16[24,2048]{1,0:T(8,128)(2,1)S(1)}, u32[]{:S(2)}, u32[]{:S(2)}) collective-permute-start(bf16[24,2048]{1,0:T(8,128)(2,1)S(1)} %pad_maximum_fusion.17), channel_id=1, source_target_pairs={{0,4},{1,5},{2,6},{3,7},{4,0},{5,1},{6,2},{7,3},{8,12},{9,13},{10,... | collective-permute-start | bytes 294920 | tf_op jit(solution)/shard_map/ppermute | solution.py:23
  334.6 10.8 %collective-permute-start.16 = (bf16[24,2048]{1,0:T(8,128)(2,1)S(1)}, bf16[24,2048]{1,0:T(8,128)(2,1)S(1)}, u32[]{:S(2)}, u32[]{:S(2)}) collective-permute-start(bf16[24,2048]{1,0:T(8,128)(2,1)S(1)} %get-tuple-element.45), channel_id=1, source_target_pairs={{0,6},{1,7},{2,0},{3,1},{4,2},{5,3},{6,4},{7,5},{8,14},{9,15},{10,... | collective-permute-start | bytes 294920 | tf_op jit(solution)/shard_map/ppermute | solution.py:23
  339.3 9.6 %collective-permute-start.17 = (bf16[24,2048]{1,0:T(8,128)(2,1)S(1)}, bf16[24,2048]{1,0:T(8,128)(2,1)S(1)}, u32[]{:S(2)}, u32[]{:S(2)}) collective-permute-start(bf16[24,2048]{1,0:T(8,128)(2,1)S(1)} %get-tuple-element.47), channel_id=1, source_target_pairs={{0,4},{1,5},{2,6},{3,7},{4,0},{5,1},{6,2},{7,3},{8,12},{9,13},{10,... | collective-permute-start | bytes 294920 | tf_op jit(solution)/shard_map/ppermute | solution.py:23
  339.3 9.6 %collective-permute-start.18 = (bf16[24,2048]{1,0:T(8,128)(2,1)S(1)}, bf16[24,2048]{1,0:T(8,128)(2,1)S(1)}, u32[]{:S(2)}, u32[]{:S(2)}) collective-permute-start(bf16[24,2048]{1,0:T(8,128)(2,1)S(1)} %get-tuple-element.46), channel_id=1, source_target_pairs={{0,2},{1,3},{2,4},{3,5},{4,6},{5,7},{6,0},{7,1},{8,10},{9,11},{10,... | collective-permute-start | bytes 294920 | tf_op jit(solution)/shard_map/ppermute | solution.py:23
  340.0 17.8 %collective-permute-start.20 = (bf16[64,4096]{1,0:T(8,128)(2,1)S(1)}, bf16[64,4096]{1,0:T(8,128)(2,1)S(1)}, u32[]{:S(2)}, u32[]{:S(2)}) collective-permute-start(bf16[64,4096]{1,0:T(8,128)(2,1)S(1)} %fusion.31), channel_id=1, source_target_pairs={{0,8},{8,16},{16,24},{1,9},{9,17},{17,25},{2,10},{10,18},{18,26},{... | collective-permute-start | bytes 1572872 | tf_op jit(solution)/shard_map/ppermute | solution.py:13
  349.2 10.0 %collective-permute-start.19 = (bf16[12,4096]{1,0:T(8,128)(2,1)S(1)}, bf16[12,4096]{1,0:T(8,128)(2,1)S(1)}, u32[]{:S(2)}, u32[]{:S(2)}) collective-permute-start(bf16[12,4096]{1,0:T(8,128)(2,1)S(1)} %fusion.88), channel_id=1, source_target_pairs={{0,8},{8,16},{16,24},{1,9},{9,17},{17,25},{2,10},{10,18},{18,26},{... | collective-permute-start | bytes 294920 | tf_op jit(solution)/shard_map/ppermute | solution.py:13
  359.7 7.4 %collective-permute-start.21 = (bf16[24,2048]{1,0:T(8,128)(2,1)S(1)}, bf16[24,2048]{1,0:T(8,128)(2,1)S(1)}, u32[]{:S(2)}, u32[]{:S(2)}) collective-permute-start(bf16[24,2048]{1,0:T(8,128)(2,1)S(1)} %pad_maximum_fusion.18), channel_id=1, source_target_pairs={{0,2},{1,3},{2,4},{3,5},{4,6},{5,7},{6,0},{7,1},{8,10},{9,11},{10,... | collective-permute-start | bytes 294920 | tf_op jit(solution)/shard_map/ppermute | solution.py:23
  362.4 7.8 %collective-permute-start.22 = (bf16[24,2048]{1,0:T(8,128)(2,1)S(1)}, bf16[24,2048]{1,0:T(8,128)(2,1)S(1)}, u32[]{:S(2)}, u32[]{:S(2)}) collective-permute-start(bf16[24,2048]{1,0:T(8,128)(2,1)S(1)} %pad_maximum_fusion.18), channel_id=1, source_target_pairs={{0,4},{1,5},{2,6},{3,7},{4,0},{5,1},{6,2},{7,3},{8,12},{9,13},{10,... | collective-permute-start | bytes 294920 | tf_op jit(solution)/shard_map/ppermute | solution.py:23
  393.5 10.0 %collective-permute-start.27 = (bf16[24,2048]{1,0:T(8,128)(2,1)S(1)}, bf16[24,2048]{1,0:T(8,128)(2,1)S(1)}, u32[]{:S(2)}, u32[]{:S(2)}) collective-permute-start(bf16[24,2048]{1,0:T(8,128)(2,1)S(1)} %get-tuple-element.42), channel_id=1, source_target_pairs={{0,4},{1,5},{2,6},{3,7},{4,0},{5,1},{6,2},{7,3},{8,12},{9,13},{10,... | collective-permute-start | bytes 294920 | tf_op jit(solution)/shard_map/ppermute | solution.py:23
  394.0 9.5 %collective-permute-start.28 = (bf16[24,2048]{1,0:T(8,128)(2,1)S(1)}, bf16[24,2048]{1,0:T(8,128)(2,1)S(1)}, u32[]{:S(2)}, u32[]{:S(2)}) collective-permute-start(bf16[24,2048]{1,0:T(8,128)(2,1)S(1)} %get-tuple-element.41), channel_id=1, source_target_pairs={{0,2},{1,3},{2,4},{3,5},{4,6},{5,7},{6,0},{7,1},{8,10},{9,11},{10,... | collective-permute-start | bytes 294920 | tf_op jit(solution)/shard_map/ppermute | solution.py:23
  (144 other events, 1536.1 us)
where the time goes:
time: 412 us; the launch traced here: 406 us
  matrix products  105 us (25%)
  starting transfers between devices  103 us (25%)
  local copies, waits for them, and re-layouts  90.9 us (22%)
  waiting for transfers between devices  72.2 us (18%)
  other arithmetic  30.9 us (8%)
    ppermute x42, starting transfers between devices, shift_chip(): lax.ppermute(block, 'dp', [(i, (i + CORES * step) % count) for i in range...  68.1 us
    ppermute x42, waiting for transfers between devices, shift_chip(): lax.ppermute(block, 'dp', [(i, (i + CORES * step) % count) for i in range...  45.2 us
    dot_general x5, local copies, waits for them, and re-layouts, per_device(): jnp.dot(hidden, down_weight, preferred_element_type=jnp.float32)  35.9 us
    ppermute x10, starting transfers between devices, shift_section(): return lax.ppermute(block, 'section', route)  32 us
    ppermute x10, waiting for transfers between devices, shift_section(): return lax.ppermute(block, 'section', route)  25.1 us
    dot_general x3, matrix products, per_device(): lax.dot_general(upstream_all, down_weight, contract_last, preferred_eleme...  18.8 us
    dot_general x3, matrix products, per_device(): jnp.dot(hidden, down_weight, preferred_element_type=jnp.float32)  18.7 us
    dot_general x3, matrix products, per_device(): lax.dot_general(grad_up, up_weight, contract_last, preferred_element_type...  18.3 us
  transfers between devices with their start and end apart: 66, of which 23 were waited for; matrix products, arithmetic and copies ran while one was open for 41% of the time, Pallas kernels for 0%

commit v1 on v0

v1 whole, which is shorter than its diff:
```python
import functools

import jax
import jax.numpy as jnp
from jax import lax
from jax.experimental import pallas as pl
from jax.experimental.pallas import tpu as pltpu
from jax.sharding import PartitionSpec as P

EPS = 1e-05
CORES = 2
CHUNK = 256
BF16 = jnp.bfloat16
F32 = jnp.float32
NN = (((1,), (0,)), ((), ()))
NT = (((1,), (1,)), ((), ()))
VMEM = pl.BlockSpec(memory_space=pltpu.VMEM)
SMEM = pl.BlockSpec(memory_space=pltpu.SMEM)


def shift_section(block, step):
    count = lax.axis_size("section")
    route = [(i - step, i) for i in range(count) if 0 <= i - step < count]
    return lax.ppermute(block, "section", route)


def swap_core(block):
    count = lax.axis_size("dp")
    return lax.ppermute(block, "dp", [(i, i ^ 1) for i in range(count)])


def shift_chip(block, step):
    count = lax.axis_size("dp")
    return lax.ppermute(block, "dp", [(i, (i + CORES * step) % count) for i in range(count)])


def gather_rows(packed):
    chips = lax.axis_size("dp") // CORES
    own = [packed] + [shift_chip(packed, j) for j in range(1, chips)]
    return own + [swap_core(block) for block in own]


def dot(a, b, dims=NN):
    return lax.dot_general(a, b, dims, preferred_element_type=F32)


def halves(column):
    rows = column.shape[0]
    wide = jnp.broadcast_to(column, (rows, 128))
    return (wide + pltpu.roll(wide, rows // 2, 0))[:, :1]


def top_rows(rows, period):
    return lax.rem(lax.broadcasted_iota(jnp.int32, (rows, 1), 0), period) < period // 2


def pick(activity, route_column):
    rows, half = route_column.shape[0], activity.shape[1] // 2
    tokens = activity.shape[0]
    hit = route_column == lax.broadcasted_iota(jnp.int32, (rows, tokens), 1)
    top = top_rows(rows, rows)
    left = jnp.where(hit & top, 1.0, 0.0).astype(BF16)
    right = jnp.where(hit & jnp.logical_not(top), 1.0, 0.0).astype(BF16)
    return dot(left, activity[:, :half]) + dot(right, activity[:, half:])


def put(activity, rows, route_row):
    tokens, half = activity.shape[0], activity.shape[1] // 2
    count = route_row.shape[1]
    hit = route_row == lax.broadcasted_iota(jnp.int32, (tokens, count), 0)
    first = lax.broadcasted_iota(jnp.int32, (tokens, count), 1) < count // 2
    left = jnp.where(hit & first, 1.0, 0.0)
    right = jnp.where(hit & jnp.logical_not(first), 1.0, 0.0)
    taken = jnp.sum(left, axis=1, keepdims=True) > 0.5
    new_left = jnp.where(taken, dot(left.astype(BF16), rows), activity[:, :half].astype(F32))
    new_right = jnp.where(taken, dot(right.astype(BF16), rows), activity[:, half:].astype(F32))
    return new_left.astype(BF16), new_right.astype(BF16)


def by_half(vector, rows):
    half = vector.shape[1] // 2
    return jnp.where(top_rows(rows, rows), vector[:, :half], vector[:, half:])


def inverse_rms(rows):
    width = 2 * rows.shape[1]
    mean = halves(jnp.sum(rows * rows, axis=1, keepdims=True)) / width
    return lax.rsqrt(mean + EPS)


def normalize(rows, gain, router):
    normed = (rows * inverse_rms(rows) * by_half(gain, rows.shape[0])).astype(BF16)
    logit = jnp.sum(normed.astype(F32) * by_half(router, rows.shape[0]), axis=1, keepdims=True)
    return normed, jax.nn.sigmoid(halves(logit))


def stack_blocks(refs, out):
    out[...] = jnp.concatenate([ref[...].astype(F32) for ref in refs], axis=0).astype(BF16)


def join_halves(left, right, period):
    rows = left.shape[0]
    top = top_rows(rows, period)
    return jnp.where(
        top,
        left + pltpu.roll(right, rows - period // 2, 0),
        right + pltpu.roll(left, period // 2, 0),
    )


def first_forward_kernel(act, column, gain, router, rows_out, normed_out, gate_out):
    rows = pick(act[...], column[...])
    normed, gate = normalize(rows, gain[...], router[...])
    rows_out[...] = rows.astype(BF16)
    normed_out[...] = normed
    gate_out[...] = jnp.broadcast_to(gate, gate_out.shape)


def first_backward_kernel(ticks, act, stash, columns, gain, rows_out, saved_out, normed_out):
    rows_out[...] = pick(act[...], columns[0]).astype(BF16)
    for k in range(ticks):
        rows = pick(stash[k], columns[k])
        saved_out[k] = rows.astype(BF16)
        count = rows.shape[0]
        normed_out[k] = (rows * inverse_rms(rows) * by_half(gain[...], count)).astype(BF16)


def source_kernel(flag, moved, fresh, column, source_out, rows_out):
    source = jnp.where(flag[0] == 1, fresh[...], moved[...])
    source_out[...] = source
    rows_out[...] = pick(source, column[...]).astype(BF16)


def select(base, moved, column, behind_row):
    rows = column.shape[0]
    hit = column == behind_row
    same = top_rows(rows, rows) == (lax.broadcasted_iota(jnp.int32, (rows, rows), 1) < rows // 2)
    match = jnp.where(hit & same, 1.0, 0.0)
    found = jnp.max(match, axis=1, keepdims=True) > 0.5
    return jnp.where(found, dot(match.astype(BF16), moved), base.astype(F32))


def next_forward_kernel(
    base, moved, column, behind_row, gain, router, rows_out, normed_out, gate_out
):
    rows = select(base[...], moved[...], column[...], behind_row[...])
    normed, gate = normalize(rows, gain[...], router[...])
    rows_out[...] = rows.astype(BF16)
    normed_out[...] = normed
    gate_out[...] = jnp.broadcast_to(gate, gate_out.shape)


def next_backward_kernel(base, moved, column, ahead_row, rows_out):
    rows_out[...] = select(base[...], moved[...], column[...], ahead_row[...]).astype(BF16)


def land_kernel(source, moved, row, out):
    half = source.shape[1] // 2
    left, right = put(source[...], moved[...], row[...])
    out[:, :half] = left
    out[:, half:] = right


def output_kernel(act, rows, row, *outs):
    out = outs[-1]
    half = act.shape[1] // 2
    left, right = put(act[...], rows[...], row[...])
    out[0, 0, :, :half] = left
    out[0, 0, :, half:] = right


def forward_kernel(count, *refs):
    blocks = refs[:count]
    up, down, own_out, cross_out, rows, total = refs[count:]
    step, steps = pl.program_id(0), pl.num_programs(0)
    period, half = blocks[0].shape

    @pl.when(step == 0)
    def _():
        stack_blocks(blocks, rows)
        total[...] = jnp.zeros_like(total)

    x = rows[...]
    top = top_rows(x.shape[0], period)
    u = join_halves(dot(x, up[:half, :]), dot(x, up[half:, :]), period)
    hidden = u * jax.nn.sigmoid(u)
    left = jnp.where(top, hidden, 0.0).astype(BF16)
    right = jnp.where(top, 0.0, hidden).astype(BF16)
    total[...] += dot(left, down[:, :half]) + dot(right, down[:, half:])

    @pl.when(step == steps - 1)
    def _():
        write_blocks(total, own_out, cross_out)


def write_blocks(total, own_out, cross_out):
    chips, period, _ = own_out.shape
    for j in range(chips):
        own_out[j] = total[j * period : (j + 1) * period, :]
        low = (chips + j) * period
        cross_out[j] = total[low : low + period, :].astype(BF16)


def backward_kernel(count, *refs):
    normed_blocks = refs[:count]
    grad_blocks = refs[count : 2 * count]
    up, down, router, term_in, own_out, cross_out, term_out, x_n, x_g, total, gate, inner = refs[
        2 * count :
    ]
    step, steps = pl.program_id(0), pl.num_programs(0)
    period, half = grad_blocks[0].shape
    all_rows = x_n.shape[0]
    top = top_rows(all_rows, period)

    @pl.when(step == 0)
    def _():
        stack_blocks(normed_blocks, x_n)
        stack_blocks(grad_blocks, x_g)
        total[...] = jnp.zeros_like(total)
        inner[...] = jnp.zeros_like(inner)
        vector = jnp.where(top, router[:, :half], router[:, half:])
        logit = jnp.sum(x_n[...].astype(F32) * vector, axis=1, keepdims=True)
        wide = jnp.broadcast_to(logit, gate.shape)
        gate[...] = jax.nn.sigmoid(join_halves(wide, wide, period))

    x = x_n[...]
    g = x_g[...]
    u = join_halves(dot(x, up[:half, :]), dot(x, up[half:, :]), period)
    grad_hidden = join_halves(dot(g, down[:, :half], NT), dot(g, down[:, half:], NT), period)
    grad_hidden = grad_hidden * gate[:, :1]
    sig = jax.nn.sigmoid(u)
    hidden = (u * sig).astype(BF16).astype(F32)
    inner[...] += jnp.sum(grad_hidden * hidden, axis=1, keepdims=True)
    grad_up = grad_hidden * sig * (1.0 + u * (1.0 - sig))
    left = jnp.where(top, grad_up, 0.0).astype(BF16)
    right = jnp.where(top, 0.0, grad_up).astype(BF16)
    total[...] += dot(left, up[:half, :], NT) + dot(right, up[half:, :], NT)

    @pl.when(step == steps - 1)
    def _():
        logit = inner[...] * (1.0 - gate[...])
        vector = jnp.where(top, router[:, :half], router[:, half:])
        total[...] += logit[:, :1] * vector
        write_blocks(total, own_out, cross_out)
        wide = logit.T[:1]
        first = lax.rem(lax.broadcasted_iota(jnp.int32, (1, all_rows), 1), period) < period // 2
        pieces = []
        rest = wide
        for _ in range(3):
            piece = rest.astype(BF16).astype(F32)
            pieces.append(piece)
            rest = rest - piece
        sums = []
        for side in (first, jnp.logical_not(first)):
            stacked = jnp.concatenate(
                [jnp.where(side, p, 0.0) for p in pieces]
                + [jnp.zeros((5, all_rows), F32)],
                axis=0,
            )
            sums.append(jnp.sum(dot(stacked.astype(BF16), x), axis=0, keepdims=True))
        term_out[...] = term_in[...] + jnp.concatenate(sums, axis=0)


def pair_kernel(own, crossed, own_out, *outs):
    own_out[...] = own[0] + crossed[0].astype(F32)
    for j, out in enumerate(outs):
        out[...] = (own[j + 1] + crossed[j + 1].astype(F32)).astype(BF16)


def forward_end_kernel(rows, gate, own, *refs):
    out = refs[-1]
    block = own[...]
    for ref in refs[:-1]:
        block = block + ref[...].astype(F32)
    out[...] = (rows[...].astype(F32) + gate[:, :1] * block).astype(BF16)


def backward_end_kernel(upstream, saved, gain, own, *refs):
    out = refs[-1]
    grad_normed = own[...]
    for ref in refs[:-1]:
        grad_normed = grad_normed + ref[...].astype(F32)
    picked = saved[...].astype(F32)
    inv_rms = inverse_rms(picked)
    scaled_grad = grad_normed * by_half(gain[...], picked.shape[0])
    unit = picked * inv_rms
    mean = halves(jnp.sum(scaled_grad * unit, axis=1, keepdims=True)) / (2 * picked.shape[1])
    grad_rows = inv_rms * (scaled_grad - unit * mean)
    out[...] = (upstream[...].astype(F32) + grad_rows).astype(BF16)


def call(kernel, outs, *operands, smem=0, **more):
    return pl.pallas_call(
        kernel,
        out_shape=outs,
        in_specs=[SMEM] * smem + [VMEM] * (len(operands) - smem),
        out_specs=jax.tree.map(lambda _: VMEM, outs),
        **more,
    )(*operands)


def shaped(shape, dtype=BF16):
    return jax.ShapeDtypeStruct(tuple(shape), dtype)


def whole(shape):
    return pl.BlockSpec(tuple(shape), lambda i: (0,) * len(shape))


def weight_call(kernel, blocks, extra, outs, scratch, up, down, matmuls):
    width, hidden = up.shape
    chunk = min(CHUNK, hidden)
    rows = len(blocks) * blocks[0].shape[0]
    return pl.pallas_call(
        kernel,
        grid=(hidden // chunk,),
        out_shape=outs,
        in_specs=[whole(b.shape) for b in blocks]
        + [
            pl.BlockSpec((width, chunk), lambda i: (0, i)),
            pl.BlockSpec((chunk, width), lambda i: (i, 0)),
        ]
        + [whole(e.shape) for e in extra],
        out_specs=[whole(o.shape) for o in outs],
        scratch_shapes=scratch,
        compiler_params=pltpu.CompilerParams(vmem_limit_bytes=40 * 2**20),
        cost_estimate=pl.CostEstimate(
            flops=2 * matmuls * rows * width * hidden,
            bytes_accessed=4 * width * hidden,
            transcendentals=rows * hidden,
        ),
    )(*blocks, up, down, *extra)


def scatter_sum(own, cross):
    chips, period, half = own.shape
    crossed = swap_core(cross)
    sums = call(
        pair_kernel,
        [shaped((period, half), F32)] + [shaped((period, half))] * (chips - 1),
        own,
        crossed,
    )
    return [sums[0]] + [shift_chip(sums[j], -j) for j in range(1, chips)]


def per_device(
    arrive, entering, stash, back_arrive, head_grad, norm_gain, router, w_up, w_down, routes
):
    section = lax.axis_index("section")
    last = lax.axis_size("section") - 1
    dp_count = lax.axis_size("dp")
    chips = dp_count // CORES
    up, down = w_up[0], w_down[0]
    slots = routes.shape[3]
    tokens, width = arrive.shape[1:]
    half = width // 2
    ticks = stash.shape[1]
    period = 2 * slots

    route = routes[0]
    twice = jnp.concatenate([route, route], axis=-1)
    columns = twice[..., None]
    columns_f = [columns[k, 0] for k in range(ticks)]
    columns_b = columns[:, 1]
    rows_of = twice[:, :, None, :]
    behind = jnp.where(section == 0, -2, shift_section(twice[:, 0], 1))
    ahead = jnp.where(section == last, -2, shift_section(twice[:, 1], -1))
    behind = jnp.where(behind < 0, -2, behind)[:, None, :]
    ahead = jnp.where(ahead < 0, -2, ahead)[:, None, :]
    at_first = (section == 0).astype(jnp.int32).reshape(1)
    at_last = (section == last).astype(jnp.int32).reshape(1)

    packed = shaped((period, half))
    gate_shape = shaped((period, 128), F32)
    part_outs = [shaped((chips, period, half), F32), shaped((chips, period, half))]
    all_rows = dp_count * period
    scratch_rows = pltpu.VMEM((all_rows, half), BF16)
    scratch_total = pltpu.VMEM((all_rows, half), F32)
    scratch_column = pltpu.VMEM((all_rows, 128), F32)

    forward_in, backward_in = arrive[0], back_arrive[0]
    forward_rows, forward_normed, gate = call(
        first_forward_kernel,
        [packed, packed, gate_shape],
        forward_in,
        columns_f[0],
        norm_gain,
        router,
    )
    backward_rows, saved, saved_normed = call(
        functools.partial(first_backward_kernel, ticks),
        [packed, shaped((ticks, period, half)), shaped((ticks, period, half))],
        backward_in,
        stash[0],
        columns_b,
        norm_gain,
    )
    term = jnp.zeros((2, half), F32)
    forward_out = backward_out = None
    out_shape = shaped((1, ticks, tokens, width))

    def write_out(result, k, act, rows, row):
        before = [] if result is None else [result]
        return pl.pallas_call(
            output_kernel,
            grid=(1,),
            out_shape=out_shape,
            in_specs=[whole(act.shape), whole(rows.shape), whole(row.shape)]
            + [pl.BlockSpec(memory_space=pl.ANY)] * len(before),
            out_specs=pl.BlockSpec((1, 1, tokens, width), lambda i: (0, k, 0, 0)),
            input_output_aliases={3: 0} if before else {},
        )(act, rows, row, *before)

    for k in range(ticks):
        if k + 1 < ticks:
            forward_base = shift_section(forward_in, 1)
            backward_base = shift_section(backward_in, -1)

        blocks = gather_rows(forward_normed)
        own, cross = weight_call(
            functools.partial(forward_kernel, dp_count),
            blocks,
            [],
            part_outs,
            [scratch_rows, scratch_total],
            up,
            down,
            2,
        )
        terms = scatter_sum(own, cross)
        forward_new = call(forward_end_kernel, packed, forward_rows, gate, *terms)

        blocks = gather_rows(saved_normed[k]) + gather_rows(backward_rows)
        own, cross, term = weight_call(
            functools.partial(backward_kernel, dp_count),
            blocks,
            [router, term],
            part_outs + [shaped((2, half), F32)],
            [scratch_rows, scratch_rows, scratch_total, scratch_column, scratch_column],
            up,
            down,
            3,
        )
        terms = scatter_sum(own, cross)
        backward_new = call(
            backward_end_kernel, packed, backward_rows, saved[k], norm_gain, *terms
        )

        forward_out = write_out(forward_out, k, forward_in, forward_new, rows_of[k, 0])
        backward_out = write_out(backward_out, k, backward_in, backward_new, rows_of[k, 1])

        if k + 1 < ticks:
            full = shaped((tokens, width))
            source, base = call(
                source_kernel,
                [full, packed],
                at_first,
                forward_base,
                entering[k],
                columns_f[k + 1],
                smem=1,
            )
            moved = shift_section(forward_new, 1)
            forward_rows, forward_normed, gate = call(
                next_forward_kernel,
                [packed, packed, gate_shape],
                base,
                moved,
                columns_f[k + 1],
                behind[k],
                norm_gain,
                router,
            )
            forward_in = call(land_kernel, full, source, moved, behind[k])

            source, base = call(
                source_kernel,
                [full, packed],
                at_last,
                backward_base,
                head_grad[k],
                columns_b[k + 1],
                smem=1,
            )
            moved = shift_section(backward_new, -1)
            backward_rows = call(
                next_backward_kernel, packed, base, moved, columns_b[k + 1], ahead[k]
            )
            backward_in = call(land_kernel, full, source, moved, ahead[k])

    pair = term + swap_core(term)
    by_distance = jnp.stack([pair] + [shift_chip(pair, j) for j in range(1, chips)], axis=0)
    chip = lax.axis_index("dp") // CORES
    total = jnp.zeros_like(pair)
    for j in range(chips):
        total = total + lax.dynamic_index_in_dim(by_distance, (chip - j) % chips, 0, False)
    scale = 1.0 / float(ticks * slots * dp_count)
    return forward_out, backward_out, total.reshape(1, width) * scale


def solution(mesh):
    in_specs = (
        P("section", "dp", None),
        P(None, "dp", None),
        P("section", None, "dp", None),
        P("section", "dp", None),
        P(None, "dp", None),
        P("section", None),
        P("section", None),
        P("section", None, "dp"),
        P("section", "dp", None),
        P("section", None, None, "dp"),
    )
    out_specs = (P("section", None, "dp", None), P("section", None, "dp", None), P("section", None))
    return jax.shard_map(
        per_device, mesh=mesh, in_specs=in_specs, out_specs=out_specs, check_vma=False
    )
```

time: 412 us -> 333 us (0.81)
  Pallas kernels: 0 us -> 127 us
  matrix products: 105 us -> 0 us
  local copies, waits for them, and re-layouts: 90.9 us -> 37.5 us
  other arithmetic: 30.9 us -> 1.02 us
  waiting for transfers between devices: 72.2 us -> 44.8 us
  starting transfers between devices: 103 us -> 119 us
    pallas_call x0 -> x38, Pallas kernels: none -> 127 us  [the longest x6 59.4 us: weight_call(): pl.pallas_call(kernel, grid=(hidden // chunk,), out_shape=outs, in_specs=...]
    dot_general x41 -> x0, matrix products: 105 us -> none  [the longest x3 18.8 us: per_device(): lax.dot_general(upstream_all, down_weight, contract_last, preferred_eleme...]
    dot_general x6 -> x0, local copies, waits for them, and re-layouts: 41.4 us -> none  [the longest x5 35.9 us: per_device(): jnp.dot(hidden, down_weight, preferred_element_type=jnp.float32)]
    ppermute x10, waiting for transfers between devices: 25.1 us -> 1.44 us  [shift_section(): return lax.ppermute(block, 'section', route)]
    unnamed x261 -> x119, local copies, waits for them, and re-layouts: 8.46 us -> 27.6 us
    transpose x9 -> x0, local copies, waits for them, and re-layouts: 12.7 us -> none  [the longest x8 12.6 us: gather_rows(): both = both.reshape(CORES * chips, 2, count, half).swapaxes(1, 2)]
    ppermute x42 -> x48, starting transfers between devices: 68.1 us -> 79.4 us  [shift_chip(): lax.ppermute(block, 'dp', [(i, (i + CORES * step) % count) for i in range...]
    another operation x27 -> x1, other arithmetic: 11 us -> 0.03 us  [per_device(): jnp.stack([pair] + [shift_chip(pair, j) for j in range(1, chips)], axis=0)]
  transfers between devices with their start and end apart: 66 -> 101, of which waited for: 23 -> 16; matrix products, arithmetic and copies ran while one was open for 41% -> 3% of each run, Pallas kernels for 0% -> 36%
where the time goes in v1:
time: 333 us; the launch traced here: 331 us
  Pallas kernels  127 us (38%)
  starting transfers between devices  119 us (36%)
  waiting for transfers between devices  44.8 us (13%)
  local copies, waits for them, and re-layouts  37.5 us (11%)
    ppermute x48, starting transfers between devices, shift_chip(): lax.ppermute(block, 'dp', [(i, (i + CORES * step) % count) for i in range...  79.4 us
    pallas_call x6, Pallas kernels, weight_call(): pl.pallas_call(kernel, grid=(hidden // chunk,), out_shape=outs, in_specs=...  59.4 us
    pallas_call x26, Pallas kernels, call(): pl.pallas_call(kernel, out_shape=outs, in_specs=[SMEM] * smem + [VMEM] *...  55 us
    ppermute x48, waiting for transfers between devices, shift_chip(): lax.ppermute(block, 'dp', [(i, (i + CORES * step) % count) for i in range...  43.3 us
    ppermute x10, starting transfers between devices, shift_section(): return lax.ppermute(block, 'section', route)  30.9 us
    unnamed x119, local copies, waits for them, and re-layouts  27.6 us
    pallas_call x6, Pallas kernels, write_out(): pl.pallas_call(output_kernel, grid=(1,), out_shape=out_shape, in_specs=[w...  13 us
    ppermute x43, starting transfers between devices, swap_core(): return lax.ppermute(block, 'dp', [(i, i ^ 1) for i in range(count)])  8.7 us
  transfers between devices with their start and end apart: 101, of which 16 were waited for; matrix products, arithmetic and copies ran while one was open for 3% of the time, Pallas kernels for 36%

profile of v1, /device:TPU:0, one launch (start us, length us, event | category | flops | bytes accessed | tf_op | source)
XLA Modules:
  0.0 331.0 jit_solution(18068681118552909787)
XLA Ops:
  2.2 2.9 shard_map.141
  6.2 3.1 collective-permute-start.39
  9.3 2.6 collective-permute-start.40
  15.0 5.2 %collective-permute-start.47 = (bf16[24,2048]{1,0:T(8,128)(2,1)S(1)}, bf16[24,2048]{1,0:T(8,128)(2,1)S(1)}, u32[]{:S(2)}, u32[]{:S(2)}) collective-permute-start(bf16[24,2048]{1,0:T(8,128)(2,1)S(1)} %copy-done.20), channel_id=1, source_target_pairs={{0,4},{1,5},{2,6},{3,7},{4,0},{5,1},{6,2},{7,3},{8,12},{9,13},{10,... | collective-permute-start | bytes 294920 | tf_op jit(solution)/shard_map/ppermute | solution.py:34
  20.2 4.1 %collective-permute-start.48 = (bf16[24,2048]{1,0:T(8,128)(2,1)S(1)}, bf16[24,2048]{1,0:T(8,128)(2,1)S(1)}, u32[]{:S(2)}, u32[]{:S(2)}) collective-permute-start(bf16[24,2048]{1,0:T(8,128)(2,1)S(1)} %copy-done.20), channel_id=1, source_target_pairs={{0,6},{1,7},{2,0},{3,1},{4,2},{5,3},{6,4},{7,5},{8,14},{9,15},{10,... | collective-permute-start | bytes 294920 | tf_op jit(solution)/shard_map/ppermute | solution.py:34
  25.0 2.3 shard_map.122
  27.9 3.3 %collective-permute-start.3 = (bf16[24,2048]{1,0:T(8,128)(2,1)}, bf16[24,2048]{1,0:T(8,128)(2,1)S(1)}, u32[]{:S(2)}, u32[]{:S(2)}) collective-permute-start(bf16[24,2048]{1,0:T(8,128)(2,1)} %get-tuple-element.65.refs_0_), channel_id=1, source_target_pairs={{0,6},{1,7},{2,0},{3,1},{4,2},{5,3},{6,4},{7,5},{8,14},{9,15},{10,... | collective-permute-start | bytes 294920 | tf_op jit(solution)/shard_map/ppermute | solution.py:34
  32.8 2.2 collective-permute-done.1.refs_1_
  35.0 3.3 collective-permute-done.2.refs_2_
  41.5 3.4 %copy-done = bf16[1,4096,1024]{2,1,0:T(8,128)(2,1)S(1)} copy-done((bf16[1,4096,1024]{2,1,0:T(8,128)(2,1)S(1)}, bf16[1,4096,1024]{2,1,0:T(8,128)(2,1)}, u32[]{:S(2)}) %copy-start) | copy-done | bytes 8388632
  44.9 12.1 %shard_map.142 = (f32[4,24,2048]{2,1,0:T(8,128)S(1)}, bf16[4,24,2048]{2,1,0:T(8,128)(2,1)S(1)}, f32[2,2048]{1,0:T(2,128)S(1)}) custom-call(bf16[24,2048]{1,0:T(8,128)(2,1)S(1)} %get-tuple-element.127.refs_0_, bf16[24,2048]{1,0:T(8,128)(2,1)S(1)} %collective-permute-done.39.refs_1_, bf16[24,2048]{1,0:T(8,128)(2,1)S(1)} %collective-permute-done.40.refs_2_, ...), custom_call_target="tpu_custom_call" | custom-call | flops 9663676416 | bytes 16777216 | tf_op jit(solution)/shard_map/pallas_call | solution.py:314
  60.0 4.2 %collective-permute-start.13 = (s32[3,24]{1,0:T(4,128)S(1)}, s32[3,24]{1,0:T(4,128)S(1)}, u32[]{:S(2)}, u32[]{:S(2)}) collective-permute-start(s32[3,24]{1,0:T(4,128)S(1)} %bitcast.95), channel_id=1, source_target_pairs={{0,8},{8,16},{16,24},{1,9},{9,17},{17,25},{2,10},{10,18},{18,26},{... | collective-permute-start | bytes 872 | tf_op jit(solution)/shard_map/ppermute | solution.py:24
  64.4 7.8 %shard_map.123 = (f32[4,24,2048]{2,1,0:T(8,128)S(1)}, bf16[4,24,2048]{2,1,0:T(8,128)(2,1)S(1)}) custom-call(bf16[24,2048]{1,0:T(8,128)(2,1)S(1)} %copy-done.17, bf16[24,2048]{1,0:T(8,128)(2,1)S(1)} %collective-permute-done.1.refs_1_, bf16[24,2048]{1,0:T(8,128)(2,1)S(1)} %collective-permute-done.2.refs_2_, ...), custom_call_target="tpu_custom_call" | custom-call | flops 3221225472 | bytes 16777216 | tf_op jit(solution)/shard_map/pallas_call | solution.py:314
  79.1 5.0 %collective-permute-start = (bf16[64,4096]{1,0:T(8,128)(2,1)S(1)}, bf16[64,4096]{1,0:T(8,128)(2,1)S(1)}, u32[]{:S(2)}, u32[]{:S(2)}) collective-permute-start(bf16[64,4096]{1,0:T(8,128)(2,1)S(1)} %bitcast.83), channel_id=1, source_target_pairs={{0,8},{8,16},{16,24},{1,9},{9,17},{17,25},{2,10},{10,18},{18,26},{... | collective-permute-start | bytes 1572872 | tf_op jit(solution)/shard_map/ppermute | solution.py:24
  89.7 2.2 collective-permute-start.10
  91.9 6.4 %collective-permute-done.55.refs_1_ = bf16[24,2048]{1,0:T(8,128)(2,1)S(1)} collective-permute-done((bf16[24,2048]{1,0:T(8,128)(2,1)}, bf16[24,2048]{1,0:T(8,128)(2,1)S(1)}, u32[]{:S(2)}, u32[]{:S(2)}) %collective-permute-start.55) | collective-permute-done | bytes 98336 | tf_op jit(solution)/shard_map/ppermute | solution.py:34
  98.3 3.8 %collective-permute-start.9 = (bf16[24,2048]{1,0:T(8,128)(2,1)}, bf16[24,2048]{1,0:T(8,128)(2,1)S(1)}, u32[]{:S(2)}, u32[]{:S(2)}) collective-permute-start(bf16[24,2048]{1,0:T(8,128)(2,1)} %get-tuple-element.69), channel_id=1, source_target_pairs={{0,6},{1,7},{2,0},{3,1},{4,2},{5,3},{6,4},{7,5},{8,14},{9,15},{10,... | collective-permute-start | bytes 294920 | tf_op jit(solution)/shard_map/ppermute | solution.py:34
  102.1 2.3 shard_map.144.rows
  113.2 4.8 %collective-permute-start.12 = (bf16[24,2048]{1,0:T(8,128)(2,1)}, bf16[24,2048]{1,0:T(8,128)(2,1)S(1)}, u32[]{:S(2)}, u32[]{:S(2)}) collective-permute-start(bf16[24,2048]{1,0:T(8,128)(2,1)} %shard_map.125.rows), channel_id=1, source_target_pairs={{0,8},{8,16},{16,24},{1,9},{9,17},{17,25},{2,10},{10,18},{18,26},{... | collective-permute-start | bytes 294920 | tf_op jit(solution)/shard_map/ppermute | solution.py:24
  128.8 2.5 collective-permute-start.68
  133.9 2.5 collective-permute-done.68.refs_10_
  136.3 2.7 collective-permute-start.17
  139.6 4.1 %collective-permute-done.16.refs_2_ = bf16[24,2048]{1,0:T(8,128)(2,1)S(1)} collective-permute-done((bf16[24,2048]{1,0:T(8,128)(2,1)}, bf16[24,2048]{1,0:T(8,128)(2,1)S(1)}, u32[]{:S(2)}, u32[]{:S(2)}) %collective-permute-start.16) | collective-permute-done | bytes 98336 | tf_op jit(solution)/shard_map/ppermute | solution.py:34
  144.8 3.4 %copy-done.2 = bf16[1,4096,1024]{2,1,0:T(8,128)(2,1)S(1)} copy-done((bf16[1,4096,1024]{2,1,0:T(8,128)(2,1)S(1)}, bf16[1,4096,1024]{2,1,0:T(8,128)(2,1)}, u32[]{:S(2)}) %copy-start.2) | copy-done | bytes 8388632
  149.0 11.9 %shard_map.148 = (f32[4,24,2048]{2,1,0:T(8,128)S(1)}, bf16[4,24,2048]{2,1,0:T(8,128)(2,1)S(1)}, f32[2,2048]{1,0:T(2,128)S(1)}) custom-call(bf16[24,2048]{1,0:T(8,128)(2,1)S(1)} %get-tuple-element.126.refs_0_, bf16[24,2048]{1,0:T(8,128)(2,1)S(1)} %collective-permute-done.60.refs_1_, bf16[24,2048]{1,0:T(8,128)(2,1)S(1)} %collective-permute-done.61.refs_2_, ...), custom_call_target="tpu_custom_call" | custom-call | flops 9663676416 | bytes 16777216 | tf_op jit(solution)/shard_map/pallas_call | solution.py:314
  162.0 3.4 %copy-done.3 = bf16[1,4096,1024]{2,1,0:T(8,128)(2,1)S(1)} copy-done((bf16[1,4096,1024]{2,1,0:T(8,128)(2,1)S(1)}, bf16[1,4096,1024]{2,1,0:T(8,128)(2,1)}, u32[]{:S(2)}) %copy-start.3) | copy-done | bytes 8388632
  165.4 7.8 %shard_map.129 = (f32[4,24,2048]{2,1,0:T(8,128)S(1)}, bf16[4,24,2048]{2,1,0:T(8,128)(2,1)S(1)}) custom-call(bf16[24,2048]{1,0:T(8,128)(2,1)S(1)} %copy-done.19, bf16[24,2048]{1,0:T(8,128)(2,1)S(1)} %collective-permute-done.15.refs_1_, bf16[24,2048]{1,0:T(8,128)(2,1)S(1)} %collective-permute-done.16.refs_2_, ...), custom_call_target="tpu_custom_call" | custom-call | flops 3221225472 | bytes 16777216 | tf_op jit(solution)/shard_map/pallas_call | solution.py:314
  180.1 5.6 %collective-permute-start.14 = (bf16[64,4096]{1,0:T(8,128)(2,1)}, bf16[64,4096]{1,0:T(8,128)(2,1)S(1)}, u32[]{:S(2)}, u32[]{:S(2)}) collective-permute-start(bf16[64,4096]{1,0:T(8,128)(2,1)} %shard_map.126.act), channel_id=1, source_target_pairs={{0,8},{8,16},{16,24},{1,9},{9,17},{17,25},{2,10},{10,18},{18,26},{... | collective-permute-start | bytes 1572872 | tf_op jit(solution)/shard_map/ppermute | solution.py:24
  188.9 3.1 collective-permute-start.75
  193.1 2.2 collective-permute-start.77
  197.4 2.3 collective-permute-start.23
  199.7 3.4 %collective-permute-done.76.refs_1_ = bf16[24,2048]{1,0:T(8,128)(2,1)S(1)} collective-permute-done((bf16[24,2048]{1,0:T(8,128)(2,1)}, bf16[24,2048]{1,0:T(8,128)(2,1)S(1)}, u32[]{:S(2)}, u32[]{:S(2)}) %collective-permute-start.76) | collective-permute-done | bytes 98336 | tf_op jit(solution)/shard_map/ppermute | solution.py:34
  203.2 2.5 collective-permute-start.25
  207.6 4.5 %collective-permute-done.24.refs_1_ = bf16[24,2048]{1,0:T(8,128)(2,1)S(1)} collective-permute-done((bf16[24,2048]{1,0:T(8,128)(2,1)}, bf16[24,2048]{1,0:T(8,128)(2,1)S(1)}, u32[]{:S(2)}, u32[]{:S(2)}) %collective-permute-start.24) | collective-permute-done | bytes 98336 | tf_op jit(solution)/shard_map/ppermute | solution.py:34
  212.1 2.3 shard_map.150.rows
  217.6 4.9 %collective-permute-start.26 = (bf16[24,2048]{1,0:T(8,128)(2,1)}, bf16[24,2048]{1,0:T(8,128)(2,1)S(1)}, u32[]{:S(2)}, u32[]{:S(2)}) collective-permute-start(bf16[24,2048]{1,0:T(8,128)(2,1)} %shard_map.131.rows), channel_id=1, source_target_pairs={{0,8},{8,16},{16,24},{1,9},{9,17},{17,25},{2,10},{10,18},{18,26},{... | collective-permute-start | bytes 294920 | tf_op jit(solution)/shard_map/ppermute | solution.py:24
  237.2 2.3 collective-permute-start.88
  240.2 3.9 %collective-permute-done.87.refs_10_ = bf16[24,2048]{1,0:T(8,128)(2,1)S(1)} collective-permute-done((bf16[24,2048]{1,0:T(8,128)(2,1)}, bf16[24,2048]{1,0:T(8,128)(2,1)S(1)}, u32[]{:S(2)}, u32[]{:S(2)}) %collective-permute-start.87) | collective-permute-done | bytes 98336 | tf_op jit(solution)/shard_map/ppermute | solution.py:34
  244.1 4.2 %collective-permute-start.29 = (bf16[24,2048]{1,0:T(8,128)(2,1)}, bf16[24,2048]{1,0:T(8,128)(2,1)S(1)}, u32[]{:S(2)}, u32[]{:S(2)}) collective-permute-start(bf16[24,2048]{1,0:T(8,128)(2,1)} %get-tuple-element.86.refs_0_), channel_id=1, source_target_pairs={{0,6},{1,7},{2,0},{3,1},{4,2},{5,3},{6,4},{7,5},{8,14},{9,15},{10,... | collective-permute-start | bytes 294920 | tf_op jit(solution)/shard_map/ppermute | solution.py:34
  248.8 3.5 %collective-permute-done.28.refs_2_ = bf16[24,2048]{1,0:T(8,128)(2,1)S(1)} collective-permute-done((bf16[24,2048]{1,0:T(8,128)(2,1)}, bf16[24,2048]{1,0:T(8,128)(2,1)S(1)}, u32[]{:S(2)}, u32[]{:S(2)}) %collective-permute-start.28) | collective-permute-done | bytes 98336 | tf_op jit(solution)/shard_map/ppermute | solution.py:34
  253.4 3.4 %copy-done.4 = bf16[1,4096,1024]{2,1,0:T(8,128)(2,1)S(1)} copy-done((bf16[1,4096,1024]{2,1,0:T(8,128)(2,1)S(1)}, bf16[1,4096,1024]{2,1,0:T(8,128)(2,1)}, u32[]{:S(2)}) %copy-start.4) | copy-done | bytes 8388632
  257.7 11.9 %shard_map.153 = (f32[4,24,2048]{2,1,0:T(8,128)S(1)}, bf16[4,24,2048]{2,1,0:T(8,128)(2,1)S(1)}, f32[2,2048]{1,0:T(2,128)S(1)}) custom-call(bf16[24,2048]{1,0:T(8,128)(2,1)S(1)} %get-tuple-element.125.refs_0_, bf16[24,2048]{1,0:T(8,128)(2,1)S(1)} %collective-permute-done.79.refs_1_, bf16[24,2048]{1,0:T(8,128)(2,1)S(1)} %collective-permute-done.80.refs_2_, ...), custom_call_target="tpu_custom_call" | custom-call | flops 9663676416 | bytes 16777216 | tf_op jit(solution)/shard_map/pallas_call | solution.py:314
  271.1 3.4 %copy-done.5 = bf16[1,4096,1024]{2,1,0:T(8,128)(2,1)S(1)} copy-done((bf16[1,4096,1024]{2,1,0:T(8,128)(2,1)S(1)}, bf16[1,4096,1024]{2,1,0:T(8,128)(2,1)}, u32[]{:S(2)}) %copy-start.5) | copy-done | bytes 8388632
  274.4 7.8 %shard_map.134 = (f32[4,24,2048]{2,1,0:T(8,128)S(1)}, bf16[4,24,2048]{2,1,0:T(8,128)(2,1)S(1)}) custom-call(bf16[24,2048]{1,0:T(8,128)(2,1)S(1)} %copy-done.18, bf16[24,2048]{1,0:T(8,128)(2,1)S(1)} %collective-permute-done.27.refs_1_, bf16[24,2048]{1,0:T(8,128)(2,1)S(1)} %collective-permute-done.28.refs_2_, ...), custom_call_target="tpu_custom_call" | custom-call | flops 3221225472 | bytes 16777216 | tf_op jit(solution)/shard_map/pallas_call | solution.py:314
  298.7 2.2 shard_map.132.act
  310.5 3.0 collective-permute-start.35
  316.0 5.1 %collective-permute-done.95.refs_1_ = bf16[24,2048]{1,0:T(8,128)(2,1)S(1)} collective-permute-done((bf16[24,2048]{1,0:T(8,128)(2,1)}, bf16[24,2048]{1,0:T(8,128)(2,1)S(1)}, u32[]{:S(2)}, u32[]{:S(2)}) %collective-permute-start.95) | collective-permute-done | bytes 98336 | tf_op jit(solution)/shard_map/ppermute | solution.py:34
  321.8 2.2 shard_map.155.rows
  (334 shorter events, 126.9 us)
Async XLA Ops:
  11.9 15.4 %collective-permute-start.41 = (bf16[24,2048]{1,0:T(8,128)(2,1)S(1)}, bf16[24,2048]{1,0:T(8,128)(2,1)S(1)}, u32[]{:S(2)}, u32[]{:S(2)}) collective-permute-start(bf16[24,2048]{1,0:T(8,128)(2,1)S(1)} %get-tuple-element.127.refs_0_), channel_id=1, source_target_pairs={{0,6},{1,7},{2,0},{3,1},{4,2},{5,3},{6,4},{7,5},{8,14},{9,15},{10,... | collective-permute-start | bytes 294920 | tf_op jit(solution)/shard_map/ppermute | solution.py:34
  13.2 14.0 %collective-permute-start.42 = (bf16[24,2048]{1,0:T(8,128)(2,1)S(1)}, bf16[24,2048]{1,0:T(8,128)(2,1)S(1)}, u32[]{:S(2)}, u32[]{:S(2)}) collective-permute-start(bf16[24,2048]{1,0:T(8,128)(2,1)S(1)} %get-tuple-element.127.refs_0_), channel_id=1, source_target_pairs={{0,1},{1,0},{2,3},{3,2},{4,5},{5,4},{6,7},{7,6},{8,9},{9,8},{10,11... | collective-permute-start | bytes 294920 | tf_op jit(solution)/shard_map/ppermute | solution.py:29
  13.3 14.1 %collective-permute-start.46 = (bf16[24,2048]{1,0:T(8,128)(2,1)}, bf16[24,2048]{1,0:T(8,128)(2,1)S(1)}, u32[]{:S(2)}, u32[]{:S(2)}) collective-permute-start(bf16[24,2048]{1,0:T(8,128)(2,1)} %get-tuple-element.94.refs_8_.upstream), channel_id=1, source_target_pairs={{0,2},{1,3},{2,4},{3,5},{4,6},{5,7},{6,0},{7,1},{8,10},{9,11},{10,... | collective-permute-start | bytes 294920 | tf_op jit(solution)/shard_map/ppermute | solution.py:34
  15.0 12.9 %collective-permute-start.47 = (bf16[24,2048]{1,0:T(8,128)(2,1)S(1)}, bf16[24,2048]{1,0:T(8,128)(2,1)S(1)}, u32[]{:S(2)}, u32[]{:S(2)}) collective-permute-start(bf16[24,2048]{1,0:T(8,128)(2,1)S(1)} %copy-done.20), channel_id=1, source_target_pairs={{0,4},{1,5},{2,6},{3,7},{4,0},{5,1},{6,2},{7,3},{8,12},{9,13},{10,... | collective-permute-start | bytes 294920 | tf_op jit(solution)/shard_map/ppermute | solution.py:34
  39.0 18.9 %collective-permute-start.4 = (bf16[24,2048]{1,0:T(8,128)(2,1)S(1)}, bf16[24,2048]{1,0:T(8,128)(2,1)S(1)}, u32[]{:S(2)}, u32[]{:S(2)}) collective-permute-start(bf16[24,2048]{1,0:T(8,128)(2,1)S(1)} %copy-done.17), channel_id=1, source_target_pairs={{0,1},{1,0},{2,3},{3,2},{4,5},{5,4},{6,7},{7,6},{8,9},{9,8},{10,11... | collective-permute-start | bytes 294920 | tf_op jit(solution)/shard_map/ppermute | solution.py:29
  39.5 39.5 %collective-permute-start.58 = (s32[3,24]{1,0:T(4,128)S(1)}, s32[3,24]{1,0:T(4,128)S(1)}, u32[]{:S(2)}, u32[]{:S(2)}) collective-permute-start(s32[3,24]{1,0:T(4,128)S(1)} %bitcast.96), channel_id=1, source_target_pairs={{8,0},{16,8},{24,16},{9,1},{17,9},{25,17},{10,2},{18,10},{26,18},{... | collective-permute-start | bytes 872 | tf_op jit(solution)/shard_map/ppermute | solution.py:24
  40.8 19.2 %collective-permute-start.5 = (bf16[24,2048]{1,0:T(8,128)(2,1)S(1)}, bf16[24,2048]{1,0:T(8,128)(2,1)S(1)}, u32[]{:S(2)}, u32[]{:S(2)}) collective-permute-start(bf16[24,2048]{1,0:T(8,128)(2,1)S(1)} %collective-permute-done.1.refs_1_), channel_id=1, source_target_pairs={{0,1},{1,0},{2,3},{3,2},{4,5},{5,4},{6,7},{7,6},{8,9},{9,8},{10,11... | collective-permute-start | bytes 294920 | tf_op jit(solution)/shard_map/ppermute | solution.py:29
  41.0 23.3 %collective-permute-start.6 = (bf16[24,2048]{1,0:T(8,128)(2,1)S(1)}, bf16[24,2048]{1,0:T(8,128)(2,1)S(1)}, u32[]{:S(2)}, u32[]{:S(2)}) collective-permute-start(bf16[24,2048]{1,0:T(8,128)(2,1)S(1)} %collective-permute-done.2.refs_2_), channel_id=1, source_target_pairs={{0,1},{1,0},{2,3},{3,2},{4,5},{5,4},{6,7},{7,6},{8,9},{9,8},{10,11... | collective-permute-start | bytes 294920 | tf_op jit(solution)/shard_map/ppermute | solution.py:29
  41.4 23.0 %collective-permute-start.7 = (bf16[24,2048]{1,0:T(8,128)(2,1)S(1)}, bf16[24,2048]{1,0:T(8,128)(2,1)S(1)}, u32[]{:S(2)}, u32[]{:S(2)}) collective-permute-start(bf16[24,2048]{1,0:T(8,128)(2,1)S(1)} %collective-permute-done.3.refs_3_), channel_id=1, source_target_pairs={{0,1},{1,0},{2,3},{3,2},{4,5},{5,4},{6,7},{7,6},{8,9},{9,8},{10,11... | collective-permute-start | bytes 294920 | tf_op jit(solution)/shard_map/ppermute | solution.py:29
  57.9 28.2 %collective-permute-start.60 = (bf16[24,2048]{1,0:T(8,128)(2,1)S(1)}, bf16[24,2048]{1,0:T(8,128)(2,1)S(1)}, u32[]{:S(2)}, u32[]{:S(2)}) collective-permute-start(bf16[24,2048]{1,0:T(8,128)(2,1)S(1)} %get-tuple-element.126.refs_0_), channel_id=1, source_target_pairs={{0,2},{1,3},{2,4},{3,5},{4,6},{5,7},{6,0},{7,1},{8,10},{9,11},{10,... | collective-permute-start | bytes 294920 | tf_op jit(solution)/shard_map/ppermute | solution.py:34
  60.0 24.0 %collective-permute-start.13 = (s32[3,24]{1,0:T(4,128)S(1)}, s32[3,24]{1,0:T(4,128)S(1)}, u32[]{:S(2)}, u32[]{:S(2)}) collective-permute-start(s32[3,24]{1,0:T(4,128)S(1)} %bitcast.95), channel_id=1, source_target_pairs={{0,8},{8,16},{16,24},{1,9},{9,17},{17,25},{2,10},{10,18},{18,26},{... | collective-permute-start | bytes 872 | tf_op jit(solution)/shard_map/ppermute | solution.py:24
  73.1 13.0 %collective-permute-start.8 = (bf16[4,24,2048]{2,1,0:T(8,128)(2,1)S(1)}, bf16[4,24,2048]{2,1,0:T(8,128)(2,1)S(1)}, u32[]{:S(2)}, u32[]{:S(2)}) collective-permute-start(bf16[4,24,2048]{2,1,0:T(8,128)(2,1)S(1)} %get-tuple-element.67), channel_id=1, source_target_pairs={{0,1},{1,0},{2,3},{3,2},{4,5},{5,4},{6,7},{7,6},{8,9},{9,8},{10,11... | collective-permute-start | bytes 1179656 | tf_op jit(solution)/shard_map/ppermute | solution.py:29
  75.7 35.5 %collective-permute-start.38 = (bf16[64,4096]{1,0:T(8,128)(2,1)S(1)}, bf16[64,4096]{1,0:T(8,128)(2,1)S(1)}, u32[]{:S(2)}, u32[]{:S(2)}) collective-permute-start(bf16[64,4096]{1,0:T(8,128)(2,1)S(1)} %bitcast.86), channel_id=1, source_target_pairs={{8,0},{16,8},{24,16},{9,1},{17,9},{25,17},{10,2},{18,10},{26,18},{... | collective-permute-start | bytes 1572872 | tf_op jit(solution)/shard_map/ppermute | solution.py:24
  79.1 32.6 %collective-permute-start = (bf16[64,4096]{1,0:T(8,128)(2,1)S(1)}, bf16[64,4096]{1,0:T(8,128)(2,1)S(1)}, u32[]{:S(2)}, u32[]{:S(2)}) collective-permute-start(bf16[64,4096]{1,0:T(8,128)(2,1)S(1)} %bitcast.83), channel_id=1, source_target_pairs={{0,8},{8,16},{16,24},{1,9},{9,17},{17,25},{2,10},{10,18},{18,26},{... | collective-permute-start | bytes 1572872 | tf_op jit(solution)/shard_map/ppermute | solution.py:24
  89.7 14.7 %collective-permute-start.10 = (bf16[24,2048]{1,0:T(8,128)(2,1)}, bf16[24,2048]{1,0:T(8,128)(2,1)S(1)}, u32[]{:S(2)}, u32[]{:S(2)}) collective-permute-start(bf16[24,2048]{1,0:T(8,128)(2,1)} %get-tuple-element.70), channel_id=1, source_target_pairs={{0,4},{1,5},{2,6},{3,7},{4,0},{5,1},{6,2},{7,3},{8,12},{9,13},{10,... | collective-permute-start | bytes 294920 | tf_op jit(solution)/shard_map/ppermute | solution.py:34
  110.2 18.6 %collective-permute-start.63 = (bf16[24,2048]{1,0:T(8,128)(2,1)S(1)}, bf16[24,2048]{1,0:T(8,128)(2,1)S(1)}, u32[]{:S(2)}, u32[]{:S(2)}) collective-permute-start(bf16[24,2048]{1,0:T(8,128)(2,1)S(1)} %get-tuple-element.126.refs_0_), channel_id=1, source_target_pairs={{0,1},{1,0},{2,3},{3,2},{4,5},{5,4},{6,7},{7,6},{8,9},{9,8},{10,11... | collective-permute-start | bytes 294920 | tf_op jit(solution)/shard_map/ppermute | solution.py:29
  111.2 20.1 %collective-permute-start.64 = (bf16[24,2048]{1,0:T(8,128)(2,1)S(1)}, bf16[24,2048]{1,0:T(8,128)(2,1)S(1)}, u32[]{:S(2)}, u32[]{:S(2)}) collective-permute-start(bf16[24,2048]{1,0:T(8,128)(2,1)S(1)} %collective-permute-done.60.refs_1_), channel_id=1, source_target_pairs={{0,1},{1,0},{2,3},{3,2},{4,5},{5,4},{6,7},{7,6},{8,9},{9,8},{10,11... | collective-permute-start | bytes 294920 | tf_op jit(solution)/shard_map/ppermute | solution.py:29
  111.2 20.6 %collective-permute-start.65 = (bf16[24,2048]{1,0:T(8,128)(2,1)S(1)}, bf16[24,2048]{1,0:T(8,128)(2,1)S(1)}, u32[]{:S(2)}, u32[]{:S(2)}) collective-permute-start(bf16[24,2048]{1,0:T(8,128)(2,1)S(1)} %collective-permute-done.61.refs_2_), channel_id=1, source_target_pairs={{0,1},{1,0},{2,3},{3,2},{4,5},{5,4},{6,7},{7,6},{8,9},{9,8},{10,11... | collective-permute-start | bytes 294920 | tf_op jit(solution)/shard_map/ppermute | solution.py:29
  111.7 20.1 %collective-permute-start.66 = (bf16[24,2048]{1,0:T(8,128)(2,1)S(1)}, bf16[24,2048]{1,0:T(8,128)(2,1)S(1)}, u32[]{:S(2)}, u32[]{:S(2)}) collective-permute-start(bf16[24,2048]{1,0:T(8,128)(2,1)S(1)} %collective-permute-done.62.refs_3_), channel_id=1, source_target_pairs={{0,1},{1,0},{2,3},{3,2},{4,5},{5,4},{6,7},{7,6},{8,9},{9,8},{10,11... | collective-permute-start | bytes 294920 | tf_op jit(solution)/shard_map/ppermute | solution.py:29
  143.7 18.2 %collective-permute-start.18 = (bf16[24,2048]{1,0:T(8,128)(2,1)}, bf16[24,2048]{1,0:T(8,128)(2,1)S(1)}, u32[]{:S(2)}, u32[]{:S(2)}) collective-permute-start(bf16[24,2048]{1,0:T(8,128)(2,1)} %get-tuple-element.76.refs_0_), channel_id=1, source_target_pairs={{0,1},{1,0},{2,3},{3,2},{4,5},{5,4},{6,7},{7,6},{8,9},{9,8},{10,11... | collective-permute-start | bytes 294920 | tf_op jit(solution)/shard_map/ppermute | solution.py:29
  143.7 18.2 %collective-permute-start.19 = (bf16[24,2048]{1,0:T(8,128)(2,1)S(1)}, bf16[24,2048]{1,0:T(8,128)(2,1)S(1)}, u32[]{:S(2)}, u32[]{:S(2)}) collective-permute-start(bf16[24,2048]{1,0:T(8,128)(2,1)S(1)} %collective-permute-done.15.refs_1_), channel_id=1, source_target_pairs={{0,1},{1,0},{2,3},{3,2},{4,5},{5,4},{6,7},{7,6},{8,9},{9,8},{10,11... | collective-permute-start | bytes 294920 | tf_op jit(solution)/shard_map/ppermute | solution.py:29
  144.2 17.7 %collective-permute-start.20 = (bf16[24,2048]{1,0:T(8,128)(2,1)S(1)}, bf16[24,2048]{1,0:T(8,128)(2,1)S(1)}, u32[]{:S(2)}, u32[]{:S(2)}) collective-permute-start(bf16[24,2048]{1,0:T(8,128)(2,1)S(1)} %collective-permute-done.16.refs_2_), channel_id=1, source_target_pairs={{0,1},{1,0},{2,3},{3,2},{4,5},{5,4},{6,7},{7,6},{8,9},{9,8},{10,11... | collective-permute-start | bytes 294920 | tf_op jit(solution)/shard_map/ppermute | solution.py:29
  144.3 17.6 %collective-permute-start.21 = (bf16[24,2048]{1,0:T(8,128)(2,1)S(1)}, bf16[24,2048]{1,0:T(8,128)(2,1)S(1)}, u32[]{:S(2)}, u32[]{:S(2)}) collective-permute-start(bf16[24,2048]{1,0:T(8,128)(2,1)S(1)} %collective-permute-done.17.refs_3_), channel_id=1, source_target_pairs={{0,1},{1,0},{2,3},{3,2},{4,5},{5,4},{6,7},{7,6},{8,9},{9,8},{10,11... | collective-permute-start | bytes 294920 | tf_op jit(solution)/shard_map/ppermute | solution.py:29
  161.9 25.0 %collective-permute-start.74 = (bf16[4,24,2048]{2,1,0:T(8,128)(2,1)S(1)}, bf16[4,24,2048]{2,1,0:T(8,128)(2,1)}, u32[]{:S(2)}, u32[]{:S(2)}) collective-permute-start(bf16[4,24,2048]{2,1,0:T(8,128)(2,1)S(1)} %get-tuple-element.107), channel_id=1, source_target_pairs={{0,1},{1,0},{2,3},{3,2},{4,5},{5,4},{6,7},{7,6},{8,9},{9,8},{10,11... | collective-permute-start | bytes 1179656 | tf_op jit(solution)/shard_map/ppermute | solution.py:29
  174.1 19.1 %collective-permute-start.22 = (bf16[4,24,2048]{2,1,0:T(8,128)(2,1)S(1)}, bf16[4,24,2048]{2,1,0:T(8,128)(2,1)S(1)}, u32[]{:S(2)}, u32[]{:S(2)}) collective-permute-start(bf16[4,24,2048]{2,1,0:T(8,128)(2,1)S(1)} %get-tuple-element.78), channel_id=1, source_target_pairs={{0,1},{1,0},{2,3},{3,2},{4,5},{5,4},{6,7},{7,6},{8,9},{9,8},{10,11... | collective-permute-start | bytes 1179656 | tf_op jit(solution)/shard_map/ppermute | solution.py:29
  176.7 45.9 %collective-permute-start.59 = (bf16[64,4096]{1,0:T(8,128)(2,1)}, bf16[64,4096]{1,0:T(8,128)(2,1)S(1)}, u32[]{:S(2)}, u32[]{:S(2)}) collective-permute-start(bf16[64,4096]{1,0:T(8,128)(2,1)} %shard_map.145.act), channel_id=1, source_target_pairs={{8,0},{16,8},{24,16},{9,1},{17,9},{25,17},{10,2},{18,10},{26,18},{... | collective-permute-start | bytes 1572872 | tf_op jit(solution)/shard_map/ppermute | solution.py:24
  180.1 43.0 %collective-permute-start.14 = (bf16[64,4096]{1,0:T(8,128)(2,1)}, bf16[64,4096]{1,0:T(8,128)(2,1)S(1)}, u32[]{:S(2)}, u32[]{:S(2)}) collective-permute-start(bf16[64,4096]{1,0:T(8,128)(2,1)} %shard_map.126.act), channel_id=1, source_target_pairs={{0,8},{8,16},{16,24},{1,9},{9,17},{17,25},{2,10},{10,18},{18,26},{... | collective-permute-start | bytes 1572872 | tf_op jit(solution)/shard_map/ppermute | solution.py:24
  217.6 13.4 %collective-permute-start.26 = (bf16[24,2048]{1,0:T(8,128)(2,1)}, bf16[24,2048]{1,0:T(8,128)(2,1)S(1)}, u32[]{:S(2)}, u32[]{:S(2)}) collective-permute-start(bf16[24,2048]{1,0:T(8,128)(2,1)} %shard_map.131.rows), channel_id=1, source_target_pairs={{0,8},{8,16},{16,24},{1,9},{9,17},{17,25},{2,10},{10,18},{18,26},{... | collective-permute-start | bytes 294920 | tf_op jit(solution)/shard_map/ppermute | solution.py:24
  222.5 12.7 %collective-permute-start.82 = (bf16[24,2048]{1,0:T(8,128)(2,1)S(1)}, bf16[24,2048]{1,0:T(8,128)(2,1)S(1)}, u32[]{:S(2)}, u32[]{:S(2)}) collective-permute-start(bf16[24,2048]{1,0:T(8,128)(2,1)S(1)} %get-tuple-element.125.refs_0_), channel_id=1, source_target_pairs={{0,1},{1,0},{2,3},{3,2},{4,5},{5,4},{6,7},{7,6},{8,9},{9,8},{10,11... | collective-permute-start | bytes 294920 | tf_op jit(solution)/shard_map/ppermute | solution.py:29
  222.6 14.6 %collective-permute-start.83 = (bf16[24,2048]{1,0:T(8,128)(2,1)S(1)}, bf16[24,2048]{1,0:T(8,128)(2,1)S(1)}, u32[]{:S(2)}, u32[]{:S(2)}) collective-permute-start(bf16[24,2048]{1,0:T(8,128)(2,1)S(1)} %collective-permute-done.79.refs_1_), channel_id=1, source_target_pairs={{0,1},{1,0},{2,3},{3,2},{4,5},{5,4},{6,7},{7,6},{8,9},{9,8},{10,11... | collective-permute-start | bytes 294920 | tf_op jit(solution)/shard_map/ppermute | solution.py:29
  223.1 16.4 %collective-permute-start.84 = (bf16[24,2048]{1,0:T(8,128)(2,1)S(1)}, bf16[24,2048]{1,0:T(8,128)(2,1)S(1)}, u32[]{:S(2)}, u32[]{:S(2)}) collective-permute-start(bf16[24,2048]{1,0:T(8,128)(2,1)S(1)} %collective-permute-done.80.refs_2_), channel_id=1, source_target_pairs={{0,1},{1,0},{2,3},{3,2},{4,5},{5,4},{6,7},{7,6},{8,9},{9,8},{10,11... | collective-permute-start | bytes 294920 | tf_op jit(solution)/shard_map/ppermute | solution.py:29
  223.2 16.3 %collective-permute-start.85 = (bf16[24,2048]{1,0:T(8,128)(2,1)S(1)}, bf16[24,2048]{1,0:T(8,128)(2,1)S(1)}, u32[]{:S(2)}, u32[]{:S(2)}) collective-permute-start(bf16[24,2048]{1,0:T(8,128)(2,1)S(1)} %collective-permute-done.81.refs_3_), channel_id=1, source_target_pairs={{0,1},{1,0},{2,3},{3,2},{4,5},{5,4},{6,7},{7,6},{8,9},{9,8},{10,11... | collective-permute-start | bytes 294920 | tf_op jit(solution)/shard_map/ppermute | solution.py:29
  239.6 12.8 %collective-permute-start.28 = (bf16[24,2048]{1,0:T(8,128)(2,1)}, bf16[24,2048]{1,0:T(8,128)(2,1)S(1)}, u32[]{:S(2)}, u32[]{:S(2)}) collective-permute-start(bf16[24,2048]{1,0:T(8,128)(2,1)} %get-tuple-element.86.refs_0_), channel_id=1, source_target_pairs={{0,4},{1,5},{2,6},{3,7},{4,0},{5,1},{6,2},{7,3},{8,12},{9,13},{10,... | collective-permute-start | bytes 294920 | tf_op jit(solution)/shard_map/ppermute | solution.py:34
  252.4 18.2 %collective-permute-start.30 = (bf16[24,2048]{1,0:T(8,128)(2,1)}, bf16[24,2048]{1,0:T(8,128)(2,1)S(1)}, u32[]{:S(2)}, u32[]{:S(2)}) collective-permute-start(bf16[24,2048]{1,0:T(8,128)(2,1)} %get-tuple-element.86.refs_0_), channel_id=1, source_target_pairs={{0,1},{1,0},{2,3},{3,2},{4,5},{5,4},{6,7},{7,6},{8,9},{9,8},{10,11... | collective-permute-start | bytes 294920 | tf_op jit(solution)/shard_map/ppermute | solution.py:29
  252.4 18.6 %collective-permute-start.31 = (bf16[24,2048]{1,0:T(8,128)(2,1)S(1)}, bf16[24,2048]{1,0:T(8,128)(2,1)S(1)}, u32[]{:S(2)}, u32[]{:S(2)}) collective-permute-start(bf16[24,2048]{1,0:T(8,128)(2,1)S(1)} %collective-permute-done.27.refs_1_), channel_id=1, source_target_pairs={{0,1},{1,0},{2,3},{3,2},{4,5},{5,4},{6,7},{7,6},{8,9},{9,8},{10,11... | collective-permute-start | bytes 294920 | tf_op jit(solution)/shard_map/ppermute | solution.py:29
  252.9 18.1 %collective-permute-start.32 = (bf16[24,2048]{1,0:T(8,128)(2,1)S(1)}, bf16[24,2048]{1,0:T(8,128)(2,1)S(1)}, u32[]{:S(2)}, u32[]{:S(2)}) collective-permute-start(bf16[24,2048]{1,0:T(8,128)(2,1)S(1)} %collective-permute-done.28.refs_2_), channel_id=1, source_target_pairs={{0,1},{1,0},{2,3},{3,2},{4,5},{5,4},{6,7},{7,6},{8,9},{9,8},{10,11... | collective-permute-start | bytes 294920 | tf_op jit(solution)/shard_map/ppermute | solution.py:29
  253.0 18.1 %collective-permute-start.33 = (bf16[24,2048]{1,0:T(8,128)(2,1)S(1)}, bf16[24,2048]{1,0:T(8,128)(2,1)S(1)}, u32[]{:S(2)}, u32[]{:S(2)}) collective-permute-start(bf16[24,2048]{1,0:T(8,128)(2,1)S(1)} %collective-permute-done.29.refs_3_), channel_id=1, source_target_pairs={{0,1},{1,0},{2,3},{3,2},{4,5},{5,4},{6,7},{7,6},{8,9},{9,8},{10,11... | collective-permute-start | bytes 294920 | tf_op jit(solution)/shard_map/ppermute | solution.py:29
  270.5 12.7 %collective-permute-start.97 = (f32[2,2048]{1,0:T(2,128)S(1)}, f32[2,2048]{1,0:T(2,128)S(1)}, u32[]{:S(2)}, u32[]{:S(2)}) collective-permute-start(f32[2,2048]{1,0:T(2,128)S(1)} %get-tuple-element.120), channel_id=1, source_target_pairs={{0,1},{1,0},{2,3},{3,2},{4,5},{5,4},{6,7},{7,6},{8,9},{9,8},{10,11... | collective-permute-start | bytes 49160 | tf_op jit(solution)/shard_map/ppermute | solution.py:29
  270.6 30.3 %collective-permute-start.93 = (bf16[4,24,2048]{2,1,0:T(8,128)(2,1)S(1)}, bf16[4,24,2048]{2,1,0:T(8,128)(2,1)S(1)}, u32[]{:S(2)}, u32[]{:S(2)}) collective-permute-start(bf16[4,24,2048]{2,1,0:T(8,128)(2,1)S(1)} %get-tuple-element.115), channel_id=1, source_target_pairs={{0,1},{1,0},{2,3},{3,2},{4,5},{5,4},{6,7},{7,6},{8,9},{9,8},{10,11... | collective-permute-start | bytes 1179656 | tf_op jit(solution)/shard_map/ppermute | solution.py:29
  283.1 24.6 %collective-permute-start.34 = (bf16[4,24,2048]{2,1,0:T(8,128)(2,1)S(1)}, bf16[4,24,2048]{2,1,0:T(8,128)(2,1)S(1)}, u32[]{:S(2)}, u32[]{:S(2)}) collective-permute-start(bf16[4,24,2048]{2,1,0:T(8,128)(2,1)S(1)} %get-tuple-element.88), channel_id=1, source_target_pairs={{0,1},{1,0},{2,3},{3,2},{4,5},{5,4},{6,7},{7,6},{8,9},{9,8},{10,11... | collective-permute-start | bytes 1179656 | tf_op jit(solution)/shard_map/ppermute | solution.py:29
  283.2 22.4 %collective-permute-start.98 = (f32[2,2048]{1,0:T(2,128)S(1)}, f32[2,2048]{1,0:T(2,128)S(1)}, u32[]{:S(2)}, u32[]{:S(2)}) collective-permute-start(f32[2,2048]{1,0:T(2,128)S(1)} %add.69), channel_id=1, source_target_pairs={{0,2},{1,3},{2,4},{3,5},{4,6},{5,7},{6,0},{7,1},{8,10},{9,11},{10,... | collective-permute-start | bytes 49160 | tf_op jit(solution)/shard_map/ppermute | solution.py:34
  284.8 20.8 %collective-permute-start.99 = (f32[2,2048]{1,0:T(2,128)S(1)}, f32[2,2048]{1,0:T(2,128)S(1)}, u32[]{:S(2)}, u32[]{:S(2)}) collective-permute-start(f32[2,2048]{1,0:T(2,128)S(1)} %add.69), channel_id=1, source_target_pairs={{0,4},{1,5},{2,6},{3,7},{4,0},{5,1},{6,2},{7,3},{8,12},{9,13},{10,... | collective-permute-start | bytes 49160 | tf_op jit(solution)/shard_map/ppermute | solution.py:34
  286.8 18.8 %collective-permute-start.100 = (f32[2,2048]{1,0:T(2,128)S(1)}, f32[2,2048]{1,0:T(2,128)S(1)}, u32[]{:S(2)}, u32[]{:S(2)}) collective-permute-start(f32[2,2048]{1,0:T(2,128)S(1)} %add.69), channel_id=1, source_target_pairs={{0,6},{1,7},{2,0},{3,1},{4,2},{5,3},{6,4},{7,5},{8,14},{9,15},{10,... | collective-permute-start | bytes 49160 | tf_op jit(solution)/shard_map/ppermute | solution.py:34
  305.7 15.4 %collective-permute-start.95 = (bf16[24,2048]{1,0:T(8,128)(2,1)}, bf16[24,2048]{1,0:T(8,128)(2,1)S(1)}, u32[]{:S(2)}, u32[]{:S(2)}) collective-permute-start(bf16[24,2048]{1,0:T(8,128)(2,1)} %get-tuple-element.118), channel_id=1, source_target_pairs={{0,4},{1,5},{2,6},{3,7},{4,0},{5,1},{6,2},{7,3},{8,12},{9,13},{10,... | collective-permute-start | bytes 294920 | tf_op jit(solution)/shard_map/ppermute | solution.py:34
  306.9 14.3 %collective-permute-start.96 = (bf16[24,2048]{1,0:T(8,128)(2,1)}, bf16[24,2048]{1,0:T(8,128)(2,1)S(1)}, u32[]{:S(2)}, u32[]{:S(2)}) collective-permute-start(bf16[24,2048]{1,0:T(8,128)(2,1)} %get-tuple-element.119), channel_id=1, source_target_pairs={{0,2},{1,3},{2,4},{3,5},{4,6},{5,7},{6,0},{7,1},{8,10},{9,11},{10,... | collective-permute-start | bytes 294920 | tf_op jit(solution)/shard_map/ppermute | solution.py:34
  310.5 15.7 %collective-permute-start.35 = (bf16[24,2048]{1,0:T(8,128)(2,1)}, bf16[24,2048]{1,0:T(8,128)(2,1)S(1)}, u32[]{:S(2)}, u32[]{:S(2)}) collective-permute-start(bf16[24,2048]{1,0:T(8,128)(2,1)} %get-tuple-element.90), channel_id=1, source_target_pairs={{0,6},{1,7},{2,0},{3,1},{4,2},{5,3},{6,4},{7,5},{8,14},{9,15},{10,... | collective-permute-start | bytes 294920 | tf_op jit(solution)/shard_map/ppermute | solution.py:34
  313.5 12.8 %collective-permute-start.36 = (bf16[24,2048]{1,0:T(8,128)(2,1)}, bf16[24,2048]{1,0:T(8,128)(2,1)S(1)}, u32[]{:S(2)}, u32[]{:S(2)}) collective-permute-start(bf16[24,2048]{1,0:T(8,128)(2,1)} %get-tuple-element.91), channel_id=1, source_target_pairs={{0,4},{1,5},{2,6},{3,7},{4,0},{5,1},{6,2},{7,3},{8,12},{9,13},{10,... | collective-permute-start | bytes 294920 | tf_op jit(solution)/shard_map/ppermute | solution.py:34
  313.5 12.8 %collective-permute-start.37 = (bf16[24,2048]{1,0:T(8,128)(2,1)}, bf16[24,2048]{1,0:T(8,128)(2,1)S(1)}, u32[]{:S(2)}, u32[]{:S(2)}) collective-permute-start(bf16[24,2048]{1,0:T(8,128)(2,1)} %get-tuple-element.92), channel_id=1, source_target_pairs={{0,2},{1,3},{2,4},{3,5},{4,6},{5,7},{6,0},{7,1},{8,10},{9,11},{10,... | collective-permute-start | bytes 294920 | tf_op jit(solution)/shard_map/ppermute | solution.py:34
  (111 other events, 841.9 us)

commit v2 on v1

v2 whole, which is shorter than its diff:
```python
import functools

import jax
import jax.numpy as jnp
from jax import lax
from jax.experimental import pallas as pl
from jax.experimental.pallas import tpu as pltpu
from jax.sharding import PartitionSpec as P

EPS = 1e-05
CORES = 2
CHUNK = 256
WEIGHTS_LIMIT = 26
BF16 = jnp.bfloat16
F32 = jnp.float32
NN = (((1,), (0,)), ((), ()))
NT = (((1,), (1,)), ((), ()))
VMEM = pl.BlockSpec(memory_space=pltpu.VMEM)
SMEM = pl.BlockSpec(memory_space=pltpu.SMEM)


def shift_section(block, step):
    count = lax.axis_size("section")
    route = [(i - step, i) for i in range(count) if 0 <= i - step < count]
    return lax.ppermute(block, "section", route)


def swap_core(block):
    count = lax.axis_size("dp")
    return lax.ppermute(block, "dp", [(i, i ^ 1) for i in range(count)])


def shift_chip(block, step):
    count = lax.axis_size("dp")
    return lax.ppermute(block, "dp", [(i, (i + CORES * step) % count) for i in range(count)])


def swap_chips(blocks):
    count = lax.axis_size("dp")
    groups = [[c + CORES * j for j in range(count // CORES)] for c in range(CORES)]
    return lax.all_to_all(blocks, "dp", 0, 0, axis_index_groups=groups)


def gather_rows(copies):
    own = swap_chips(copies)
    return [own, swap_core(own)]


def dot(a, b, dims=NN):
    return lax.dot_general(a, b, dims, preferred_element_type=F32)


def halves(column):
    rows = column.shape[0]
    wide = jnp.broadcast_to(column, (rows, 128))
    return (wide + pltpu.roll(wide, rows // 2, 0))[:, :1]


def top_rows(rows, period):
    return lax.rem(lax.broadcasted_iota(jnp.int32, (rows, 1), 0), period) < period // 2


def pick(activity, route_column):
    rows, half = route_column.shape[0], activity.shape[1] // 2
    tokens = activity.shape[0]
    hit = route_column == lax.broadcasted_iota(jnp.int32, (rows, tokens), 1)
    top = top_rows(rows, rows)
    left = jnp.where(hit & top, 1.0, 0.0).astype(BF16)
    right = jnp.where(hit & jnp.logical_not(top), 1.0, 0.0).astype(BF16)
    return dot(left, activity[:, :half]) + dot(right, activity[:, half:])


def put(activity, rows, route_row):
    tokens, half = activity.shape[0], activity.shape[1] // 2
    count = route_row.shape[1]
    hit = route_row == lax.broadcasted_iota(jnp.int32, (tokens, count), 0)
    first = lax.broadcasted_iota(jnp.int32, (tokens, count), 1) < count // 2
    left = jnp.where(hit & first, 1.0, 0.0)
    right = jnp.where(hit & jnp.logical_not(first), 1.0, 0.0)
    taken = jnp.sum(left, axis=1, keepdims=True) > 0.5
    new_left = jnp.where(taken, dot(left.astype(BF16), rows), activity[:, :half].astype(F32))
    new_right = jnp.where(taken, dot(right.astype(BF16), rows), activity[:, half:].astype(F32))
    return new_left.astype(BF16), new_right.astype(BF16)


def by_half(vector, rows):
    half = vector.shape[1] // 2
    return jnp.where(top_rows(rows, rows), vector[:, :half], vector[:, half:])


def inverse_rms(rows):
    width = 2 * rows.shape[1]
    mean = halves(jnp.sum(rows * rows, axis=1, keepdims=True)) / width
    return lax.rsqrt(mean + EPS)


def normalize(rows, gain, router):
    normed = (rows * inverse_rms(rows) * by_half(gain, rows.shape[0])).astype(BF16)
    logit = jnp.sum(normed.astype(F32) * by_half(router, rows.shape[0]), axis=1, keepdims=True)
    return normed, jax.nn.sigmoid(halves(logit))


def stack_blocks(refs, place, out):
    blocks = [ref[(j, *place)].astype(F32) for ref in refs for j in range(ref.shape[0])]
    out[...] = jnp.concatenate(blocks, axis=0).astype(BF16)


def copies_of(out, rows, place=()):
    for j in range(out.shape[0]):
        out[(j, *place)] = rows


def join_halves(left, right, period):
    rows = left.shape[0]
    top = top_rows(rows, period)
    return jnp.where(
        top,
        left + pltpu.roll(right, rows - period // 2, 0),
        right + pltpu.roll(left, period // 2, 0),
    )


def first_forward_kernel(act, column, gain, router, rows_out, normed_out, gate_out):
    rows = pick(act[...], column[...])
    normed, gate = normalize(rows, gain[...], router[...])
    rows_out[...] = rows.astype(BF16)
    copies_of(normed_out, normed)
    gate_out[...] = jnp.broadcast_to(gate, gate_out.shape)


def first_backward_kernel(ticks, act, stash, columns, gain, rows_out, saved_out, copies_out):
    upstream = pick(act[...], columns[0]).astype(BF16)
    rows_out[...] = upstream
    copies_of(copies_out, upstream, (ticks,))
    for k in range(ticks):
        rows = pick(stash[k], columns[k])
        saved_out[k] = rows.astype(BF16)
        count = rows.shape[0]
        normed = (rows * inverse_rms(rows) * by_half(gain[...], count)).astype(BF16)
        copies_of(copies_out, normed, (k,))


def source_kernel(flag, moved, fresh, column, source_out, rows_out):
    source = jnp.where(flag[0] == 1, fresh[...], moved[...])
    source_out[...] = source
    rows_out[...] = pick(source, column[...]).astype(BF16)


def select(base, moved, column, behind_row):
    rows = column.shape[0]
    hit = column == behind_row
    same = top_rows(rows, rows) == (lax.broadcasted_iota(jnp.int32, (rows, rows), 1) < rows // 2)
    match = jnp.where(hit & same, 1.0, 0.0)
    found = jnp.max(match, axis=1, keepdims=True) > 0.5
    return jnp.where(found, dot(match.astype(BF16), moved), base.astype(F32))


def next_forward_kernel(
    base, moved, column, behind_row, gain, router, rows_out, normed_out, gate_out
):
    rows = select(base[...], moved[...], column[...], behind_row[...])
    normed, gate = normalize(rows, gain[...], router[...])
    rows_out[...] = rows.astype(BF16)
    copies_of(normed_out, normed)
    gate_out[...] = jnp.broadcast_to(gate, gate_out.shape)


def next_backward_kernel(base, moved, column, ahead_row, rows_out, copies_out):
    rows = select(base[...], moved[...], column[...], ahead_row[...]).astype(BF16)
    rows_out[...] = rows
    copies_of(copies_out, rows)


def land_kernel(source, moved, row, out):
    half = source.shape[1] // 2
    left, right = put(source[...], moved[...], row[...])
    out[:, :half] = left
    out[:, half:] = right


def output_kernel(act, rows, row, *outs):
    out = outs[-1]
    half = act.shape[1] // 2
    left, right = put(act[...], rows[...], row[...])
    out[0, 0, :, :half] = left
    out[0, 0, :, half:] = right


def forward_kernel(near, far, up, down, own_out, cross_out, rows, total):
    period, half = near.shape[1:]
    hidden_count = up.shape[1]
    chunk = min(CHUNK, hidden_count)
    stack_blocks([near, far], (), rows)
    x = rows[...]
    top = top_rows(x.shape[0], period)
    for low in range(0, hidden_count, chunk):
        n = slice(low, low + chunk)
        u = join_halves(dot(x, up[:half, n]), dot(x, up[half:, n]), period)
        hidden = u * jax.nn.sigmoid(u)
        left = jnp.where(top, hidden, 0.0).astype(BF16)
        right = jnp.where(top, 0.0, hidden).astype(BF16)
        part = dot(left, down[n, :half]) + dot(right, down[n, half:])
        total[...] = part if low == 0 else total[...] + part
    write_blocks(total, own_out, cross_out)


def write_blocks(total, own_out, cross_out):
    chips, period, _ = own_out.shape
    for j in range(chips):
        own_out[j] = total[j * period : (j + 1) * period, :]
        low = (chips + j) * period
        cross_out[j] = total[low : low + period, :].astype(BF16)


def backward_kernel(
    normed_place,
    grad_place,
    near_n,
    far_n,
    near_g,
    far_g,
    up,
    down,
    router,
    term_in,
    own_out,
    cross_out,
    term_out,
    x_n,
    x_g,
    total,
):
    period, half = own_out.shape[1:]
    all_rows = x_n.shape[0]
    hidden_count = up.shape[1]
    chunk = min(CHUNK, hidden_count)
    top = top_rows(all_rows, period)
    stack_blocks([near_n, far_n], normed_place, x_n)
    stack_blocks([near_g, far_g], grad_place, x_g)
    x = x_n[...]
    g = x_g[...]
    vector = jnp.where(top, router[:, :half], router[:, half:])
    logit = jnp.sum(x.astype(F32) * vector, axis=1, keepdims=True)
    wide = jnp.broadcast_to(logit, (all_rows, 128))
    gate = jax.nn.sigmoid(join_halves(wide, wide, period))
    inner = jnp.zeros((all_rows, 1), F32)
    for low in range(0, hidden_count, chunk):
        n = slice(low, low + chunk)
        u = join_halves(dot(x, up[:half, n]), dot(x, up[half:, n]), period)
        grad_hidden = join_halves(
            dot(g, down[n, :half], NT), dot(g, down[n, half:], NT), period
        )
        grad_hidden = grad_hidden * gate[:, :1]
        sig = jax.nn.sigmoid(u)
        hidden = (u * sig).astype(BF16).astype(F32)
        inner = inner + jnp.sum(grad_hidden * hidden, axis=1, keepdims=True)
        grad_up = grad_hidden * sig * (1.0 + u * (1.0 - sig))
        left = jnp.where(top, grad_up, 0.0).astype(BF16)
        right = jnp.where(top, 0.0, grad_up).astype(BF16)
        part = dot(left, up[:half, n], NT) + dot(right, up[half:, n], NT)
        total[...] = part if low == 0 else total[...] + part

    logit = inner * (1.0 - gate)
    total[...] += logit[:, :1] * vector
    write_blocks(total, own_out, cross_out)
    rest = logit.T[:1]
    first = lax.rem(lax.broadcasted_iota(jnp.int32, (1, all_rows), 1), period) < period // 2
    pieces = []
    for _ in range(3):
        piece = rest.astype(BF16).astype(F32)
        pieces.append(piece)
        rest = rest - piece
    sums = []
    for side in (first, jnp.logical_not(first)):
        stacked = jnp.concatenate(
            [jnp.where(side, p, 0.0) for p in pieces] + [jnp.zeros((5, all_rows), F32)], axis=0
        )
        sums.append(jnp.sum(dot(stacked.astype(BF16), x), axis=0, keepdims=True))
    term_out[...] = term_in[...] + jnp.concatenate(sums, axis=0)


def pair_kernel(own, crossed, out):
    out[...] = (own[...] + crossed[...].astype(F32)).astype(BF16)


def forward_end_kernel(rows, gate, terms, out):
    block = jnp.sum(terms[...].astype(F32), axis=0)
    out[...] = (rows[...].astype(F32) + gate[:, :1] * block).astype(BF16)


def backward_end_kernel(tick, upstream, saved, gain, terms, out):
    grad_normed = jnp.sum(terms[...].astype(F32), axis=0)
    picked = saved[tick].astype(F32)
    inv_rms = inverse_rms(picked)
    scaled_grad = grad_normed * by_half(gain[...], picked.shape[0])
    unit = picked * inv_rms
    mean = halves(jnp.sum(scaled_grad * unit, axis=1, keepdims=True)) / (2 * picked.shape[1])
    grad_rows = inv_rms * (scaled_grad - unit * mean)
    out[...] = (upstream[...].astype(F32) + grad_rows).astype(BF16)


def call(kernel, outs, *operands, smem=0, limit=8, scratch=(), cost=None):
    return pl.pallas_call(
        kernel,
        out_shape=outs,
        in_specs=[SMEM] * smem + [VMEM] * (len(operands) - smem),
        out_specs=jax.tree.map(lambda _: VMEM, outs),
        scratch_shapes=scratch,
        compiler_params=pltpu.CompilerParams(vmem_limit_bytes=limit * 2**20),
        cost_estimate=cost,
    )(*operands)


def shaped(shape, dtype=BF16):
    return jax.ShapeDtypeStruct(tuple(shape), dtype)


def whole(shape):
    return pl.BlockSpec(tuple(shape), lambda i: (0,) * len(shape))


def cost_of(matmuls, rows, weight):
    size = weight.shape[0] * weight.shape[1]
    return pl.CostEstimate(
        flops=4 * matmuls * rows * size,
        bytes_accessed=4 * size,
        transcendentals=rows * weight.shape[1],
    )


def scatter_sum(own, cross):
    return swap_chips(call(pair_kernel, shaped(own.shape), own, swap_core(cross)))


def per_device(
    arrive, entering, stash, back_arrive, head_grad, norm_gain, router, w_up, w_down, routes
):
    section = lax.axis_index("section")
    last = lax.axis_size("section") - 1
    dp_count = lax.axis_size("dp")
    chips = dp_count // CORES
    up, down = w_up[0], w_down[0]
    slots = routes.shape[3]
    tokens, width = arrive.shape[1:]
    half = width // 2
    ticks = stash.shape[1]
    period = 2 * slots

    route = routes[0]
    twice = jnp.concatenate([route, route], axis=-1)
    columns = twice[..., None]
    columns_f = [columns[k, 0] for k in range(ticks)]
    columns_b = columns[:, 1]
    rows_of = twice[:, :, None, :]
    behind = jnp.where(section == 0, -2, shift_section(twice[:, 0], 1))
    ahead = jnp.where(section == last, -2, shift_section(twice[:, 1], -1))
    behind = jnp.where(behind < 0, -2, behind)[:, None, :]
    ahead = jnp.where(ahead < 0, -2, ahead)[:, None, :]
    at_first = (section == 0).astype(jnp.int32).reshape(1)
    at_last = (section == last).astype(jnp.int32).reshape(1)

    packed = shaped((period, half))
    gate_shape = shaped((period, 128), F32)
    copies = shaped((chips, period, half))
    part_outs = [shaped((chips, period, half), F32), shaped((chips, period, half))]
    all_rows = dp_count * period
    scratch_rows = pltpu.VMEM((all_rows, half), BF16)
    scratch_total = pltpu.VMEM((all_rows, half), F32)

    forward_in, backward_in = arrive[0], back_arrive[0]
    forward_rows, forward_normed, gate = call(
        first_forward_kernel,
        [packed, copies, gate_shape],
        forward_in,
        columns_f[0],
        norm_gain,
        router,
    )
    backward_rows, saved, saved_copies = call(
        functools.partial(first_backward_kernel, ticks),
        [packed, shaped((ticks, period, half)), shaped((chips, ticks + 1, period, half))],
        backward_in,
        stash[0],
        columns_b,
        norm_gain,
        limit=16,
    )
    term = jnp.zeros((2, half), F32)
    forward_out = backward_out = None
    out_shape = shaped((1, ticks, tokens, width))

    def write_out(result, k, act, rows, row):
        before = [] if result is None else [result]
        return pl.pallas_call(
            output_kernel,
            grid=(1,),
            out_shape=out_shape,
            in_specs=[whole(act.shape), whole(rows.shape), whole(row.shape)]
            + [pl.BlockSpec(memory_space=pl.ANY)] * len(before),
            out_specs=pl.BlockSpec((1, 1, tokens, width), lambda i: (0, k, 0, 0)),
            input_output_aliases={3: 0} if before else {},
            compiler_params=pltpu.CompilerParams(vmem_limit_bytes=8 * 2**20),
        )(act, rows, row, *before)

    for k in range(ticks):
        if k + 1 < ticks:
            forward_base = shift_section(forward_in, 1)
            backward_base = shift_section(backward_in, -1)

        own, cross = call(
            forward_kernel,
            part_outs,
            *gather_rows(forward_normed),
            up,
            down,
            limit=WEIGHTS_LIMIT,
            scratch=[scratch_rows, scratch_total],
            cost=cost_of(2, all_rows, up),
        )
        terms = scatter_sum(own, cross)
        forward_new = call(forward_end_kernel, packed, forward_rows, gate, terms)

        if k == 0:
            saved_all = gather_rows(saved_copies)
            grads, place = saved_all, (ticks,)
        else:
            grads, place = gather_rows(backward_copies), ()
        own, cross, term = call(
            functools.partial(backward_kernel, (k,), place),
            part_outs + [shaped((2, half), F32)],
            *saved_all,
            *grads,
            up,
            down,
            router,
            term,
            limit=WEIGHTS_LIMIT,
            scratch=[scratch_rows, scratch_rows, scratch_total],
            cost=cost_of(3, all_rows, up),
        )
        terms = scatter_sum(own, cross)
        backward_new = call(
            functools.partial(backward_end_kernel, k),
            packed,
            backward_rows,
            saved,
            norm_gain,
            terms,
        )

        forward_out = write_out(forward_out, k, forward_in, forward_new, rows_of[k, 0])
        backward_out = write_out(backward_out, k, backward_in, backward_new, rows_of[k, 1])

        if k + 1 < ticks:
            full = shaped((tokens, width))
            source, base = call(
                source_kernel,
                [full, packed],
                at_first,
                forward_base,
                entering[k],
                columns_f[k + 1],
                smem=1,
            )
            moved = shift_section(forward_new, 1)
            forward_rows, forward_normed, gate = call(
                next_forward_kernel,
                [packed, copies, gate_shape],
                base,
                moved,
                columns_f[k + 1],
                behind[k],
                norm_gain,
                router,
            )
            forward_in = call(land_kernel, full, source, moved, behind[k])

            source, base = call(
                source_kernel,
                [full, packed],
                at_last,
                backward_base,
                head_grad[k],
                columns_b[k + 1],
                smem=1,
            )
            moved = shift_section(backward_new, -1)
            backward_rows, backward_copies = call(
                next_backward_kernel,
                [packed, copies],
                base,
                moved,
                columns_b[k + 1],
                ahead[k],
            )
            backward_in = call(land_kernel, full, source, moved, ahead[k])

    pair = term + swap_core(term)
    by_distance = jnp.stack([pair] + [shift_chip(pair, j) for j in range(1, chips)], axis=0)
    chip = lax.axis_index("dp") // CORES
    total = jnp.zeros_like(pair)
    for j in range(chips):
        total = total + lax.dynamic_index_in_dim(by_distance, (chip - j) % chips, 0, False)
    scale = 1.0 / float(ticks * slots * dp_count)
    return forward_out, backward_out, total.reshape(1, width) * scale


def solution(mesh):
    in_specs = (
        P("section", "dp", None),
        P(None, "dp", None),
        P("section", None, "dp", None),
        P("section", "dp", None),
        P(None, "dp", None),
        P("section", None),
        P("section", None),
        P("section", None, "dp"),
        P("section", "dp", None),
        P("section", None, None, "dp"),
    )
    out_specs = (P("section", None, "dp", None), P("section", None, "dp", None), P("section", None))
    return jax.shard_map(
        per_device, mesh=mesh, in_specs=in_specs, out_specs=out_specs, check_vma=False
    )
```

time: 333 us -> 339 us (1.018); the launches traced: 331 us -> 333 us
  Pallas kernels: 127 us -> 76.4 us
  local copies, waits for them, and re-layouts: 37.5 us -> 72.1 us
  waiting for transfers between devices: 44.8 us -> 78.6 us
  starting transfers between devices: 119 us -> 100 us
    ppermute x48 -> x3, starting transfers between devices: 79.4 us -> 5.9 us  [shift_chip(): lax.ppermute(block, 'dp', [(i, (i + CORES * step) % count) for i in range...]
    pallas_call x6 -> x0, Pallas kernels: 59.4 us -> none  [weight_call(): pl.pallas_call(kernel, grid=(hidden // chunk,), out_shape=outs, in_specs=...]
    all_to_all x0 -> x12, starting transfers between devices: none -> 54.8 us  [swap_chips(): return lax.all_to_all(blocks, 'dp', 0, 0, axis_index_groups=groups)]
    all_to_all x0 -> x12, waiting for transfers between devices: none -> 46.5 us  [swap_chips(): return lax.all_to_all(blocks, 'dp', 0, 0, axis_index_groups=groups)]
    ppermute x48 -> x3, waiting for transfers between devices: 43.3 us -> 0.01 us  [shift_chip(): lax.ppermute(block, 'dp', [(i, (i + CORES * step) % count) for i in range...]
    unnamed x119 -> x145, local copies, waits for them, and re-layouts: 27.6 us -> 64.9 us
    ppermute x10, waiting for transfers between devices: 1.44 us -> 24.2 us  [shift_section(): return lax.ppermute(block, 'section', route)]
    pallas_call x26 -> x32, Pallas kernels: 55 us -> 68.1 us  [call(): pl.pallas_call(kernel, out_shape=outs, in_specs=[SMEM] * smem + [VMEM] *...]
  transfers between devices with their start and end apart: 101 -> 38, of which waited for: 16 -> 16; matrix products, arithmetic and copies ran while one was open for 3% -> 3% of each run, Pallas kernels for 36% -> 22%
where the time goes in v2:
time: 339 us; the launch traced here: 333 us
  starting transfers between devices  100 us (29%)
  waiting for transfers between devices  78.6 us (23%)
  Pallas kernels  76.4 us (23%)
  local copies, waits for them, and re-layouts  72.1 us (21%)
  other arithmetic  4.06 us (1%)
    pallas_call x32, Pallas kernels, call(): pl.pallas_call(kernel, out_shape=outs, in_specs=[SMEM] * smem + [VMEM] *...  68.1 us
    unnamed x145, local copies, waits for them, and re-layouts  64.9 us
    all_to_all x12, starting transfers between devices, swap_chips(): return lax.all_to_all(blocks, 'dp', 0, 0, axis_index_groups=groups)  54.8 us
    all_to_all x12, waiting for transfers between devices, swap_chips(): return lax.all_to_all(blocks, 'dp', 0, 0, axis_index_groups=groups)  46.5 us
    ppermute x10, starting transfers between devices, shift_section(): return lax.ppermute(block, 'section', route)  37.7 us
    ppermute x10, waiting for transfers between devices, shift_section(): return lax.ppermute(block, 'section', route)  24.2 us
    pallas_call x6, Pallas kernels, write_out(): pl.pallas_call(output_kernel, grid=(1,), out_shape=out_shape, in_specs=[w...  8.32 us
    ppermute x13, waiting for transfers between devices, swap_core(): return lax.ppermute(block, 'dp', [(i, i ^ 1) for i in range(count)])  7.94 us
  transfers between devices with their start and end apart: 38, of which 16 were waited for; matrix products, arithmetic and copies ran while one was open for 3% of the time, Pallas kernels for 22%

profile of v2, /device:TPU:0, one launch (start us, length us, event | category | flops | bytes accessed | tf_op | source)
XLA Modules:
  0.0 332.8 jit_solution(8964677005598459232)
XLA Ops:
  6.5 6.3 %all-to-all-start = ((bf16[4,24,2048]{2,1,0:T(8,128)(2,1)}), bf16[4,24,2048]{2,1,0:T(8,128)(2,1)S(1)}, u32[]{:S(2)}, u32[]{:S(2)}) async-start(bf16[4,24,2048]{2,1,0:T(8,128)(2,1)} %get-tuple-element.45), calls=%async_computation | async-start | bytes 786432 | tf_op jit(solution)/shard_map/all_to_all | solution.py:41
  16.8 7.6 %all-to-all-done.near = bf16[4,24,2048]{2,1,0:T(8,128)(2,1)S(1)} async-done(((bf16[4,24,2048]{2,1,0:T(8,128)(2,1)}), bf16[4,24,2048]{2,1,0:T(8,128)(2,1)S(1)}, u32[]{:S(2)}, u32[]{:S(2)}) %all-to-all-start) | async-done | bytes 393248 | tf_op jit(solution)/shard_map/all_to_all | solution.py:41
  24.5 4.4 %all-to-all-start.6 = ((bf16[4,4,24,2048]{3,2,1,0:T(8,128)(2,1)}), bf16[4,4,24,2048]{3,2,1,0:T(8,128)(2,1)}, u32[]{:S(2)}, u32[]{:S(2)}) async-start(bf16[4,4,24,2048]{3,2,1,0:T(8,128)(2,1)} %get-tuple-element.64), calls=%async_computation.6 | async-start | bytes 3145728 | tf_op jit(solution)/shard_map/all_to_all | solution.py:41
  30.6 3.4 %copy-done.51 = bf16[1,4096,1024]{2,1,0:T(8,128)(2,1)S(1)} copy-done((bf16[1,4096,1024]{2,1,0:T(8,128)(2,1)S(1)}, bf16[1,4096,1024]{2,1,0:T(8,128)(2,1)}, u32[]{:S(2)}) %copy-start.51) | copy-done | bytes 8388632
  34.0 3.4 %copy-done.57 = bf16[1,1024,4096]{2,1,0:T(8,128)(2,1)S(1)} copy-done((bf16[1,1024,4096]{2,1,0:T(8,128)(2,1)S(1)}, bf16[1,1024,4096]{2,1,0:T(8,128)(2,1)}, u32[]{:S(2)}) %copy-start.57) | copy-done | bytes 8388632
  37.4 4.9 %shard_map.123 = (f32[4,24,2048]{2,1,0:T(8,128)S(1)}, bf16[4,24,2048]{2,1,0:T(8,128)(2,1)}) custom-call(bf16[4,24,2048]{2,1,0:T(8,128)(2,1)S(1)} %all-to-all-done.near, bf16[4,24,2048]{2,1,0:T(8,128)(2,1)S(1)} %collective-permute-done.1.far, bf16[4096,1024]{1,0:T(8,128)(2,1)S(1)} %bitcast.64, bf16[1024,4096]{1,0:T(8,128)(2,1)S(1)} %bitcast.70), custom_call_target="tpu_custom_call" | custom-call | flops 6442450944 | bytes 16777216 | tf_op jit(solution)/shard_map/pallas_call | solution.py:303
  42.4 22.7 %all-to-all-done.6.near_n.near_g = bf16[4,4,24,2048]{3,2,1,0:T(8,128)(2,1)} async-done(((bf16[4,4,24,2048]{3,2,1,0:T(8,128)(2,1)}), bf16[4,4,24,2048]{3,2,1,0:T(8,128)(2,1)}, u32[]{:S(2)}, u32[]{:S(2)}) %all-to-all-start.6) | async-done | bytes 1572896 | tf_op jit(solution)/shard_map/all_to_all | solution.py:41
  65.1 3.4 %collective-permute-start = (bf16[64,4096]{1,0:T(8,128)(2,1)S(1)}, bf16[64,4096]{1,0:T(8,128)(2,1)S(1)}, u32[]{:S(2)}, u32[]{:S(2)}) collective-permute-start(bf16[64,4096]{1,0:T(8,128)(2,1)S(1)} %bitcast.58), channel_id=1, source_target_pairs={{0,8},{8,16},{16,24},{1,9},{9,17},{17,25},{2,10},{10,18},{18,26},{... | collective-permute-start | bytes 1572872 | tf_op jit(solution)/shard_map/ppermute | solution.py:25
  69.2 3.4 %collective-permute-start.4 = (s32[3,24]{1,0:T(4,128)S(1)}, s32[3,24]{1,0:T(4,128)S(1)}, u32[]{:S(2)}, u32[]{:S(2)}) collective-permute-start(s32[3,24]{1,0:T(4,128)S(1)} %bitcast.82), channel_id=1, source_target_pairs={{0,8},{8,16},{16,24},{1,9},{9,17},{17,25},{2,10},{10,18},{18,26},{... | collective-permute-start | bytes 872 | tf_op jit(solution)/shard_map/ppermute | solution.py:25
  73.4 3.6 %all-to-all-start.1 = ((bf16[4,24,2048]{2,1,0:T(8,128)(2,1)}), bf16[4,24,2048]{2,1,0:T(8,128)(2,1)S(1)}, u32[]{:S(2)}, u32[]{:S(2)}) async-start(bf16[4,24,2048]{2,1,0:T(8,128)(2,1)} %shard_map.124), calls=%async_computation.1 | async-start | bytes 786432 | tf_op jit(solution)/shard_map/all_to_all | solution.py:41
  80.9 8.1 %all-to-all-done.1.terms = bf16[4,24,2048]{2,1,0:T(8,128)(2,1)S(1)} async-done(((bf16[4,24,2048]{2,1,0:T(8,128)(2,1)}), bf16[4,24,2048]{2,1,0:T(8,128)(2,1)S(1)}, u32[]{:S(2)}, u32[]{:S(2)}) %all-to-all-start.1) | async-done | bytes 393248 | tf_op jit(solution)/shard_map/all_to_all | solution.py:41
  89.8 3.4 %collective-permute-start.3 = (bf16[24,2048]{1,0:T(8,128)(2,1)S(1)}, bf16[24,2048]{1,0:T(8,128)(2,1)S(1)}, u32[]{:S(2)}, u32[]{:S(2)}) collective-permute-start(bf16[24,2048]{1,0:T(8,128)(2,1)S(1)} %shard_map.125.rows), channel_id=1, source_target_pairs={{0,8},{8,16},{16,24},{1,9},{9,17},{17,25},{2,10},{10,18},{18,26},{... | collective-permute-start | bytes 294920 | tf_op jit(solution)/shard_map/ppermute | solution.py:25
  98.5 3.5 %all-to-all-start.2 = ((bf16[4,24,2048]{2,1,0:T(8,128)(2,1)}), bf16[4,24,2048]{2,1,0:T(8,128)(2,1)S(1)}, u32[]{:S(2)}, u32[]{:S(2)}) async-start(bf16[4,24,2048]{2,1,0:T(8,128)(2,1)} %get-tuple-element.52), calls=%async_computation.2 | async-start | bytes 786432 | tf_op jit(solution)/shard_map/all_to_all | solution.py:41
  102.0 3.4 %copy-done.52 = bf16[1,4096,1024]{2,1,0:T(8,128)(2,1)S(1)} copy-done((bf16[1,4096,1024]{2,1,0:T(8,128)(2,1)S(1)}, bf16[1,4096,1024]{2,1,0:T(8,128)(2,1)}, u32[]{:S(2)}) %copy-start.52) | copy-done | bytes 8388632
  105.3 3.4 %copy-done.58 = bf16[1,1024,4096]{2,1,0:T(8,128)(2,1)S(1)} copy-done((bf16[1,1024,4096]{2,1,0:T(8,128)(2,1)S(1)}, bf16[1,1024,4096]{2,1,0:T(8,128)(2,1)}, u32[]{:S(2)}) %copy-start.58) | copy-done | bytes 8388632
  108.7 11.0 %shard_map.142 = (f32[4,24,2048]{2,1,0:T(8,128)S(1)}, bf16[4,24,2048]{2,1,0:T(8,128)(2,1)S(1)}, f32[2,2048]{1,0:T(2,128)S(1)}) custom-call(bf16[4,4,24,2048]{3,2,1,0:T(8,128)(2,1)} %all-to-all-done.6.near_n.near_g, bf16[4,4,24,2048]{3,2,1,0:T(8,128)(2,1)} %collective-permute-done.12.far_n.far_g, bf16[4,4,24,2048]{3,2,1,0:T(8,128)(2,1)} %all-to-all-done.6.near_n.near_g, ...), custom_call_target="tpu_custom_call" | custom-call | flops 9663676416 | bytes 16777216 | tf_op jit(solution)/shard_map/pallas_call | solution.py:303
  124.3 5.1 %all-to-all-start.7 = ((bf16[4,24,2048]{2,1,0:T(8,128)(2,1)}), bf16[4,24,2048]{2,1,0:T(8,128)(2,1)S(1)}, u32[]{:S(2)}, u32[]{:S(2)}) async-start(bf16[4,24,2048]{2,1,0:T(8,128)(2,1)} %shard_map.143), calls=%async_computation.7 | async-start | bytes 786432 | tf_op jit(solution)/shard_map/all_to_all | solution.py:41
  130.9 5.9 %collective-permute-done.15 = s32[3,24]{1,0:T(4,128)S(1)} collective-permute-done((s32[3,24]{1,0:T(4,128)S(1)}, s32[3,24]{1,0:T(4,128)S(1)}, u32[]{:S(2)}, u32[]{:S(2)}) %collective-permute-start.15) | collective-permute-done | bytes 320 | tf_op jit(solution)/shard_map/ppermute | solution.py:25
  137.4 4.3 %all-to-all-done.7.terms = bf16[4,24,2048]{2,1,0:T(8,128)(2,1)S(1)} async-done(((bf16[4,24,2048]{2,1,0:T(8,128)(2,1)}), bf16[4,24,2048]{2,1,0:T(8,128)(2,1)S(1)}, u32[]{:S(2)}, u32[]{:S(2)}) %all-to-all-start.7) | async-done | bytes 393248 | tf_op jit(solution)/shard_map/all_to_all | solution.py:41
  147.9 3.4 %collective-permute-done.14.moved = bf16[24,2048]{1,0:T(8,128)(2,1)S(1)} collective-permute-done((bf16[24,2048]{1,0:T(8,128)(2,1)S(1)}, bf16[24,2048]{1,0:T(8,128)(2,1)S(1)}, u32[]{:S(2)}, u32[]{:S(2)}) %collective-permute-start.14) | collective-permute-done | bytes 98336 | tf_op jit(solution)/shard_map/ppermute | solution.py:25
  153.4 3.5 %all-to-all-start.8 = ((bf16[4,24,2048]{2,1,0:T(8,128)(2,1)}), bf16[4,24,2048]{2,1,0:T(8,128)(2,1)S(1)}, u32[]{:S(2)}, u32[]{:S(2)}) async-start(bf16[4,24,2048]{2,1,0:T(8,128)(2,1)} %copy-done.21), calls=%async_computation.8 | async-start | bytes 786432 | tf_op jit(solution)/shard_map/all_to_all | solution.py:41
  156.9 3.4 %copy-done.53 = bf16[1,4096,1024]{2,1,0:T(8,128)(2,1)S(1)} copy-done((bf16[1,4096,1024]{2,1,0:T(8,128)(2,1)S(1)}, bf16[1,4096,1024]{2,1,0:T(8,128)(2,1)}, u32[]{:S(2)}) %copy-start.53) | copy-done | bytes 8388632
  160.3 3.4 %copy-done.59 = bf16[1,1024,4096]{2,1,0:T(8,128)(2,1)S(1)} copy-done((bf16[1,1024,4096]{2,1,0:T(8,128)(2,1)S(1)}, bf16[1,1024,4096]{2,1,0:T(8,128)(2,1)}, u32[]{:S(2)}) %copy-start.59) | copy-done | bytes 8388632
  163.6 5.1 %shard_map.129 = (f32[4,24,2048]{2,1,0:T(8,128)S(1)}, bf16[4,24,2048]{2,1,0:T(8,128)(2,1)S(1)}) custom-call(bf16[4,24,2048]{2,1,0:T(8,128)(2,1)S(1)} %copy-done.18, bf16[4,24,2048]{2,1,0:T(8,128)(2,1)} %collective-permute-done.6.far, bf16[4096,1024]{1,0:T(8,128)(2,1)S(1)} %bitcast.66, bf16[1024,4096]{1,0:T(8,128)(2,1)S(1)} %bitcast.72), custom_call_target="tpu_custom_call" | custom-call | flops 6442450944 | bytes 16777216 | tf_op jit(solution)/shard_map/pallas_call | solution.py:303
  171.4 5.0 %all-to-all-start.3 = ((bf16[4,24,2048]{2,1,0:T(8,128)(2,1)}), bf16[4,24,2048]{2,1,0:T(8,128)(2,1)S(1)}, u32[]{:S(2)}, u32[]{:S(2)}) async-start(bf16[4,24,2048]{2,1,0:T(8,128)(2,1)} %shard_map.130), calls=%async_computation.3 | async-start | bytes 786432 | tf_op jit(solution)/shard_map/all_to_all | solution.py:41
  179.3 5.7 %collective-permute-start.5 = (bf16[64,4096]{1,0:T(8,128)(2,1)S(1)}, bf16[64,4096]{1,0:T(8,128)(2,1)}, u32[]{:S(2)}, u32[]{:S(2)}) collective-permute-start(bf16[64,4096]{1,0:T(8,128)(2,1)S(1)} %shard_map.126.act), channel_id=1, source_target_pairs={{0,8},{8,16},{16,24},{1,9},{9,17},{17,25},{2,10},{10,18},{18,26},{... | collective-permute-start | bytes 1572872 | tf_op jit(solution)/shard_map/ppermute | solution.py:25
  184.9 3.5 %all-to-all-done.3.terms = bf16[4,24,2048]{2,1,0:T(8,128)(2,1)S(1)} async-done(((bf16[4,24,2048]{2,1,0:T(8,128)(2,1)}), bf16[4,24,2048]{2,1,0:T(8,128)(2,1)S(1)}, u32[]{:S(2)}, u32[]{:S(2)}) %all-to-all-start.3) | async-done | bytes 393248 | tf_op jit(solution)/shard_map/all_to_all | solution.py:41
  190.0 5.6 %collective-permute-start.8 = (bf16[24,2048]{1,0:T(8,128)(2,1)}, bf16[24,2048]{1,0:T(8,128)(2,1)}, u32[]{:S(2)}, u32[]{:S(2)}) collective-permute-start(bf16[24,2048]{1,0:T(8,128)(2,1)} %shard_map.131.rows), channel_id=1, source_target_pairs={{0,8},{8,16},{16,24},{1,9},{9,17},{17,25},{2,10},{10,18},{18,26},{... | collective-permute-start | bytes 294920 | tf_op jit(solution)/shard_map/ppermute | solution.py:25
  198.5 2.1 shard_map.133
  201.2 4.8 %all-to-all-start.4 = ((bf16[4,24,2048]{2,1,0:T(8,128)(2,1)}), bf16[4,24,2048]{2,1,0:T(8,128)(2,1)}, u32[]{:S(2)}, u32[]{:S(2)}) async-start(bf16[4,24,2048]{2,1,0:T(8,128)(2,1)} %get-tuple-element.58), calls=%async_computation.4 | async-start | bytes 786432 | tf_op jit(solution)/shard_map/all_to_all | solution.py:41
  206.0 3.4 %copy-done.54 = bf16[1,4096,1024]{2,1,0:T(8,128)(2,1)S(1)} copy-done((bf16[1,4096,1024]{2,1,0:T(8,128)(2,1)S(1)}, bf16[1,4096,1024]{2,1,0:T(8,128)(2,1)}, u32[]{:S(2)}) %copy-start.54) | copy-done | bytes 8388632
  209.4 3.4 %copy-done.60 = bf16[1,1024,4096]{2,1,0:T(8,128)(2,1)S(1)} copy-done((bf16[1,1024,4096]{2,1,0:T(8,128)(2,1)S(1)}, bf16[1,1024,4096]{2,1,0:T(8,128)(2,1)}, u32[]{:S(2)}) %copy-start.60) | copy-done | bytes 8388632
  213.5 10.0 %shard_map.148 = (f32[4,24,2048]{2,1,0:T(8,128)S(1)}, bf16[4,24,2048]{2,1,0:T(8,128)(2,1)S(1)}, f32[2,2048]{1,0:T(2,128)S(1)}) custom-call(bf16[4,4,24,2048]{3,2,1,0:T(8,128)(2,1)} %all-to-all-done.6.near_n.near_g, bf16[4,4,24,2048]{3,2,1,0:T(8,128)(2,1)} %collective-permute-done.12.far_n.far_g, bf16[4,24,2048]{2,1,0:T(8,128)(2,1)S(1)} %copy-done.20, ...), custom_call_target="tpu_custom_call" | custom-call | flops 9663676416 | bytes 16777216 | tf_op jit(solution)/shard_map/pallas_call | solution.py:303
  226.2 5.1 %all-to-all-start.9 = ((bf16[4,24,2048]{2,1,0:T(8,128)(2,1)}), bf16[4,24,2048]{2,1,0:T(8,128)(2,1)S(1)}, u32[]{:S(2)}, u32[]{:S(2)}) async-start(bf16[4,24,2048]{2,1,0:T(8,128)(2,1)} %copy-done.5), calls=%async_computation.9 | async-start | bytes 786432 | tf_op jit(solution)/shard_map/all_to_all | solution.py:41
  233.5 10.7 %collective-permute-start.16 = (bf16[64,4096]{1,0:T(8,128)(2,1)S(1)}, bf16[64,4096]{1,0:T(8,128)(2,1)}, u32[]{:S(2)}, u32[]{:S(2)}) collective-permute-start(bf16[64,4096]{1,0:T(8,128)(2,1)S(1)} %shard_map.145.act), channel_id=1, source_target_pairs={{8,0},{16,8},{24,16},{9,1},{17,9},{25,17},{10,2},{18,10},{26,18},{... | collective-permute-start | bytes 1572872 | tf_op jit(solution)/shard_map/ppermute | solution.py:25
  247.6 12.6 %collective-permute-done.16.moved = bf16[64,4096]{1,0:T(8,128)(2,1)} collective-permute-done((bf16[64,4096]{1,0:T(8,128)(2,1)S(1)}, bf16[64,4096]{1,0:T(8,128)(2,1)}, u32[]{:S(2)}, u32[]{:S(2)}) %collective-permute-start.16) | collective-permute-done | bytes 524320 | tf_op jit(solution)/shard_map/ppermute | solution.py:25
  264.0 5.1 %all-to-all-start.10 = ((bf16[4,24,2048]{2,1,0:T(8,128)(2,1)}), bf16[4,24,2048]{2,1,0:T(8,128)(2,1)}, u32[]{:S(2)}, u32[]{:S(2)}) async-start(bf16[4,24,2048]{2,1,0:T(8,128)(2,1)} %get-tuple-element.76), calls=%async_computation.10 | async-start | bytes 786432 | tf_op jit(solution)/shard_map/all_to_all | solution.py:41
  269.1 3.4 %copy-done.55 = bf16[1,4096,1024]{2,1,0:T(8,128)(2,1)S(1)} copy-done((bf16[1,4096,1024]{2,1,0:T(8,128)(2,1)S(1)}, bf16[1,4096,1024]{2,1,0:T(8,128)(2,1)}, u32[]{:S(2)}) %copy-start.55) | copy-done | bytes 8388632
  272.5 3.4 %copy-done.61 = bf16[1,1024,4096]{2,1,0:T(8,128)(2,1)S(1)} copy-done((bf16[1,1024,4096]{2,1,0:T(8,128)(2,1)S(1)}, bf16[1,1024,4096]{2,1,0:T(8,128)(2,1)}, u32[]{:S(2)}) %copy-start.61) | copy-done | bytes 8388632
  275.9 6.0 %shard_map.134 = (f32[4,24,2048]{2,1,0:T(8,128)S(1)}, bf16[4,24,2048]{2,1,0:T(8,128)(2,1)}) custom-call(bf16[4,24,2048]{2,1,0:T(8,128)(2,1)} %all-to-all-done.4.near, bf16[4,24,2048]{2,1,0:T(8,128)(2,1)} %collective-permute-done.9.far, bf16[4096,1024]{1,0:T(8,128)(2,1)S(1)} %bitcast.68, bf16[1024,4096]{1,0:T(8,128)(2,1)S(1)} %bitcast.74), custom_call_target="tpu_custom_call" | custom-call | flops 6442450944 | bytes 16777216 | tf_op jit(solution)/shard_map/pallas_call | solution.py:303
  285.7 5.1 %all-to-all-start.5 = ((bf16[4,24,2048]{2,1,0:T(8,128)(2,1)}), bf16[4,24,2048]{2,1,0:T(8,128)(2,1)S(1)}, u32[]{:S(2)}, u32[]{:S(2)}) async-start(bf16[4,24,2048]{2,1,0:T(8,128)(2,1)} %shard_map.135), calls=%async_computation.5 | async-start | bytes 786432 | tf_op jit(solution)/shard_map/all_to_all | solution.py:41
  290.8 3.4 %copy-done.56 = bf16[1,4096,1024]{2,1,0:T(8,128)(2,1)S(1)} copy-done((bf16[1,4096,1024]{2,1,0:T(8,128)(2,1)S(1)}, bf16[1,4096,1024]{2,1,0:T(8,128)(2,1)}, u32[]{:S(2)}) %copy-start.56) | copy-done | bytes 8388632
  294.2 3.4 %copy-done.62 = bf16[1,1024,4096]{2,1,0:T(8,128)(2,1)S(1)} copy-done((bf16[1,1024,4096]{2,1,0:T(8,128)(2,1)S(1)}, bf16[1,1024,4096]{2,1,0:T(8,128)(2,1)}, u32[]{:S(2)}) %copy-start.62) | copy-done | bytes 8388632
  297.6 10.1 %shard_map.153 = (f32[4,24,2048]{2,1,0:T(8,128)S(1)}, bf16[4,24,2048]{2,1,0:T(8,128)(2,1)S(1)}, f32[2,2048]{1,0:T(2,128)S(1)}) custom-call(bf16[4,4,24,2048]{3,2,1,0:T(8,128)(2,1)} %all-to-all-done.6.near_n.near_g, bf16[4,4,24,2048]{3,2,1,0:T(8,128)(2,1)} %collective-permute-done.12.far_n.far_g, bf16[4,24,2048]{2,1,0:T(8,128)(2,1)} %all-to-all-done.10.near_g, ...), custom_call_target="tpu_custom_call" | custom-call | flops 9663676416 | bytes 16777216 | tf_op jit(solution)/shard_map/pallas_call | solution.py:303
  309.6 2.1 collective-permute-start.23
  311.7 2.4 collective-permute-start.24
  316.3 3.5 %all-to-all-start.11 = ((bf16[4,24,2048]{2,1,0:T(8,128)(2,1)}), bf16[4,24,2048]{2,1,0:T(8,128)(2,1)S(1)}, u32[]{:S(2)}, u32[]{:S(2)}) async-start(bf16[4,24,2048]{2,1,0:T(8,128)(2,1)} %copy-done.4), calls=%async_computation.11 | async-start | bytes 786432 | tf_op jit(solution)/shard_map/all_to_all | solution.py:41
  327.1 2.0 shard_map.157.outs_0_
  (232 shorter events, 80.2 us)
Async XLA Ops:
  6.5 18.0 %copy-start.38 = (bf16[24,2048]{1,0:T(8,128)(2,1)}, bf16[24,2048]{1,0:T(8,128)(2,1)S(1)}, u32[]{:S(2)}) copy-start(bf16[24,2048]{1,0:T(8,128)(2,1)S(1)} %get-tuple-element.43.rows) | copy-start | bytes 294916
  6.5 18.0 %copy-start.44 = (f32[24,128]{1,0:T(8,128)}, f32[24,128]{1,0:T(8,128)S(1)}, u32[]{:S(2)}) copy-start(f32[24,128]{1,0:T(8,128)S(1)} %get-tuple-element.44.gate) | copy-start | bytes 36868
  6.5 18.0 %all-to-all-start = ((bf16[4,24,2048]{2,1,0:T(8,128)(2,1)}), bf16[4,24,2048]{2,1,0:T(8,128)(2,1)S(1)}, u32[]{:S(2)}, u32[]{:S(2)}) async-start(bf16[4,24,2048]{2,1,0:T(8,128)(2,1)} %get-tuple-element.45), calls=%async_computation | async-start | bytes 786432 | tf_op jit(solution)/shard_map/all_to_all | solution.py:41
  24.5 40.6 %all-to-all-start.6 = ((bf16[4,4,24,2048]{3,2,1,0:T(8,128)(2,1)}), bf16[4,4,24,2048]{3,2,1,0:T(8,128)(2,1)}, u32[]{:S(2)}, u32[]{:S(2)}) async-start(bf16[4,4,24,2048]{3,2,1,0:T(8,128)(2,1)} %get-tuple-element.64), calls=%async_computation.6 | async-start | bytes 3145728 | tf_op jit(solution)/shard_map/all_to_all | solution.py:41
  28.8 1.8 collective-permute-start.1
  37.4 27.7 %copy-start.1 = (bf16[1,64,4096]{2,1,0:T(8,128)(2,1)S(1)}, bf16[1,64,4096]{2,1,0:T(8,128)(2,1)}, u32[]{:S(2)}) copy-start(bf16[1,64,4096]{2,1,0:T(8,128)(2,1)} %param.10) | copy-start | bytes 1572868
  37.4 31.1 %copy-start.67 = (s32[1,3,2,12]{3,2,1,0:T(2,128)S(1)}, s32[1,3,2,12]{3,2,1,0:T(2,128)}, u32[]{:S(2)}) copy-start(s32[1,3,2,12]{3,2,1,0:T(2,128)} %param.19) | copy-start | bytes 868
  42.3 30.3 %collective-permute-start.2 = (bf16[4,24,2048]{2,1,0:T(8,128)(2,1)}, bf16[4,24,2048]{2,1,0:T(8,128)(2,1)S(1)}, u32[]{:S(2)}, u32[]{:S(2)}) collective-permute-start(bf16[4,24,2048]{2,1,0:T(8,128)(2,1)} %get-tuple-element.47), channel_id=1, source_target_pairs={{0,1},{1,0},{2,3},{3,2},{4,5},{5,4},{6,7},{7,6},{8,9},{9,8},{10,11... | collective-permute-start | bytes 1179656 | tf_op jit(solution)/shard_map/ppermute | solution.py:30
  65.1 36.9 %collective-permute-start.12 = (bf16[4,4,24,2048]{3,2,1,0:T(8,128)(2,1)}, bf16[4,4,24,2048]{3,2,1,0:T(8,128)(2,1)}, u32[]{:S(2)}, u32[]{:S(2)}) collective-permute-start(bf16[4,4,24,2048]{3,2,1,0:T(8,128)(2,1)} %all-to-all-done.6.near_n.near_g), channel_id=1, source_target_pairs={{0,1},{1,0},{2,3},{3,2},{4,5},{5,4},{6,7},{7,6},{8,9},{9,8},{10,11... | collective-permute-start | bytes 4718600 | tf_op jit(solution)/shard_map/ppermute | solution.py:30
  65.1 28.9 %collective-permute-start = (bf16[64,4096]{1,0:T(8,128)(2,1)S(1)}, bf16[64,4096]{1,0:T(8,128)(2,1)S(1)}, u32[]{:S(2)}, u32[]{:S(2)}) collective-permute-start(bf16[64,4096]{1,0:T(8,128)(2,1)S(1)} %bitcast.58), channel_id=1, source_target_pairs={{0,8},{8,16},{16,24},{1,9},{9,17},{17,25},{2,10},{10,18},{18,26},{... | collective-permute-start | bytes 1572872 | tf_op jit(solution)/shard_map/ppermute | solution.py:25
  69.2 11.2 %collective-permute-start.4 = (s32[3,24]{1,0:T(4,128)S(1)}, s32[3,24]{1,0:T(4,128)S(1)}, u32[]{:S(2)}, u32[]{:S(2)}) collective-permute-start(s32[3,24]{1,0:T(4,128)S(1)} %bitcast.82), channel_id=1, source_target_pairs={{0,8},{8,16},{16,24},{1,9},{9,17},{17,25},{2,10},{10,18},{18,26},{... | collective-permute-start | bytes 872 | tf_op jit(solution)/shard_map/ppermute | solution.py:25
  73.4 15.6 %all-to-all-start.1 = ((bf16[4,24,2048]{2,1,0:T(8,128)(2,1)}), bf16[4,24,2048]{2,1,0:T(8,128)(2,1)S(1)}, u32[]{:S(2)}, u32[]{:S(2)}) async-start(bf16[4,24,2048]{2,1,0:T(8,128)(2,1)} %shard_map.124), calls=%async_computation.1 | async-start | bytes 786432 | tf_op jit(solution)/shard_map/all_to_all | solution.py:41
  77.0 18.5 %copy-start.8 = (f32[1,4096]{1,0:T(1,128)S(1)}, f32[1,4096]{1,0:T(1,128)}, u32[]{:S(2)}) copy-start(f32[1,4096]{1,0:T(1,128)} %gain.13) | copy-start | bytes 49156
  77.0 18.4 %copy-start.27 = (f32[1,4096]{1,0:T(1,128)S(1)}, f32[1,4096]{1,0:T(1,128)}, u32[]{:S(2)}) copy-start(f32[1,4096]{1,0:T(1,128)} %router.11) | copy-start | bytes 49156
  89.8 5.6 %collective-permute-start.3 = (bf16[24,2048]{1,0:T(8,128)(2,1)S(1)}, bf16[24,2048]{1,0:T(8,128)(2,1)S(1)}, u32[]{:S(2)}, u32[]{:S(2)}) collective-permute-start(bf16[24,2048]{1,0:T(8,128)(2,1)S(1)} %shard_map.125.rows), channel_id=1, source_target_pairs={{0,8},{8,16},{16,24},{1,9},{9,17},{17,25},{2,10},{10,18},{18,26},{... | collective-permute-start | bytes 294920 | tf_op jit(solution)/shard_map/ppermute | solution.py:25
  94.0 25.7 %copy-start.47 = (s32[1,24]{1,0:T(1,128)}, s32[1,24]{1,0:T(1,128)S(1)}, u32[]{:S(2)}) copy-start(s32[1,24]{1,0:T(1,128)S(1)} %get-tuple-element.103.row.behind_row) | copy-start | bytes 292
  98.5 25.1 %all-to-all-start.2 = ((bf16[4,24,2048]{2,1,0:T(8,128)(2,1)}), bf16[4,24,2048]{2,1,0:T(8,128)(2,1)S(1)}, u32[]{:S(2)}, u32[]{:S(2)}) async-start(bf16[4,24,2048]{2,1,0:T(8,128)(2,1)} %get-tuple-element.52), calls=%async_computation.2 | async-start | bytes 786432 | tf_op jit(solution)/shard_map/all_to_all | solution.py:41
  119.7 3.0 collective-permute-start.13
  119.8 26.0 %collective-permute-start.11 = (bf16[64,4096]{1,0:T(8,128)(2,1)S(1)}, bf16[64,4096]{1,0:T(8,128)(2,1)}, u32[]{:S(2)}, u32[]{:S(2)}) collective-permute-start(bf16[64,4096]{1,0:T(8,128)(2,1)S(1)} %bitcast.61), channel_id=1, source_target_pairs={{8,0},{16,8},{24,16},{9,1},{17,9},{25,17},{10,2},{18,10},{26,18},{... | collective-permute-start | bytes 1572872 | tf_op jit(solution)/shard_map/ppermute | solution.py:25
  121.1 15.7 %collective-permute-start.15 = (s32[3,24]{1,0:T(4,128)S(1)}, s32[3,24]{1,0:T(4,128)S(1)}, u32[]{:S(2)}, u32[]{:S(2)}) collective-permute-start(s32[3,24]{1,0:T(4,128)S(1)} %bitcast.81), channel_id=1, source_target_pairs={{8,0},{16,8},{24,16},{9,1},{17,9},{25,17},{10,2},{18,10},{26,18},{... | collective-permute-start | bytes 872 | tf_op jit(solution)/shard_map/ppermute | solution.py:25
  124.3 17.4 %all-to-all-start.7 = ((bf16[4,24,2048]{2,1,0:T(8,128)(2,1)}), bf16[4,24,2048]{2,1,0:T(8,128)(2,1)S(1)}, u32[]{:S(2)}, u32[]{:S(2)}) async-start(bf16[4,24,2048]{2,1,0:T(8,128)(2,1)} %shard_map.143), calls=%async_computation.7 | async-start | bytes 786432 | tf_op jit(solution)/shard_map/all_to_all | solution.py:41
  130.7 26.1 %collective-permute-start.6 = (bf16[4,24,2048]{2,1,0:T(8,128)(2,1)}, bf16[4,24,2048]{2,1,0:T(8,128)(2,1)}, u32[]{:S(2)}, u32[]{:S(2)}) collective-permute-start(bf16[4,24,2048]{2,1,0:T(8,128)(2,1)} %copy-done.17), channel_id=1, source_target_pairs={{0,1},{1,0},{2,3},{3,2},{4,5},{5,4},{6,7},{7,6},{8,9},{9,8},{10,11... | collective-permute-start | bytes 1179656 | tf_op jit(solution)/shard_map/ppermute | solution.py:30
  143.0 8.3 %collective-permute-start.14 = (bf16[24,2048]{1,0:T(8,128)(2,1)S(1)}, bf16[24,2048]{1,0:T(8,128)(2,1)S(1)}, u32[]{:S(2)}, u32[]{:S(2)}) collective-permute-start(bf16[24,2048]{1,0:T(8,128)(2,1)S(1)} %shard_map.144.rows), channel_id=1, source_target_pairs={{8,0},{16,8},{24,16},{9,1},{17,9},{25,17},{10,2},{18,10},{26,18},{... | collective-permute-start | bytes 294920 | tf_op jit(solution)/shard_map/ppermute | solution.py:25
  153.4 18.0 %all-to-all-start.8 = ((bf16[4,24,2048]{2,1,0:T(8,128)(2,1)}), bf16[4,24,2048]{2,1,0:T(8,128)(2,1)S(1)}, u32[]{:S(2)}, u32[]{:S(2)}) async-start(bf16[4,24,2048]{2,1,0:T(8,128)(2,1)} %copy-done.21), calls=%async_computation.8 | async-start | bytes 786432 | tf_op jit(solution)/shard_map/all_to_all | solution.py:41
  168.8 1.8 collective-permute-start.7
  171.4 17.0 %all-to-all-start.3 = ((bf16[4,24,2048]{2,1,0:T(8,128)(2,1)}), bf16[4,24,2048]{2,1,0:T(8,128)(2,1)S(1)}, u32[]{:S(2)}, u32[]{:S(2)}) async-start(bf16[4,24,2048]{2,1,0:T(8,128)(2,1)} %shard_map.130), calls=%async_computation.3 | async-start | bytes 786432 | tf_op jit(solution)/shard_map/all_to_all | solution.py:41
  179.3 17.1 %collective-permute-start.5 = (bf16[64,4096]{1,0:T(8,128)(2,1)S(1)}, bf16[64,4096]{1,0:T(8,128)(2,1)}, u32[]{:S(2)}, u32[]{:S(2)}) collective-permute-start(bf16[64,4096]{1,0:T(8,128)(2,1)S(1)} %shard_map.126.act), channel_id=1, source_target_pairs={{0,8},{8,16},{16,24},{1,9},{9,17},{17,25},{2,10},{10,18},{18,26},{... | collective-permute-start | bytes 1572872 | tf_op jit(solution)/shard_map/ppermute | solution.py:25
  184.9 21.1 %collective-permute-start.17 = (bf16[4,24,2048]{2,1,0:T(8,128)(2,1)}, bf16[4,24,2048]{2,1,0:T(8,128)(2,1)}, u32[]{:S(2)}, u32[]{:S(2)}) collective-permute-start(bf16[4,24,2048]{2,1,0:T(8,128)(2,1)} %copy-done.19), channel_id=1, source_target_pairs={{0,1},{1,0},{2,3},{3,2},{4,5},{5,4},{6,7},{7,6},{8,9},{9,8},{10,11... | collective-permute-start | bytes 1179656 | tf_op jit(solution)/shard_map/ppermute | solution.py:30
  190.0 8.4 %collective-permute-start.8 = (bf16[24,2048]{1,0:T(8,128)(2,1)}, bf16[24,2048]{1,0:T(8,128)(2,1)}, u32[]{:S(2)}, u32[]{:S(2)}) collective-permute-start(bf16[24,2048]{1,0:T(8,128)(2,1)} %shard_map.131.rows), channel_id=1, source_target_pairs={{0,8},{8,16},{16,24},{1,9},{9,17},{17,25},{2,10},{10,18},{18,26},{... | collective-permute-start | bytes 294920 | tf_op jit(solution)/shard_map/ppermute | solution.py:25
  201.2 22.3 %copy-start.40 = (f32[24,128]{1,0:T(8,128)}, f32[24,128]{1,0:T(8,128)S(1)}, u32[]{:S(2)}) copy-start(f32[24,128]{1,0:T(8,128)S(1)} %get-tuple-element.57.gate) | copy-start | bytes 36868
  201.2 25.0 %all-to-all-start.4 = ((bf16[4,24,2048]{2,1,0:T(8,128)(2,1)}), bf16[4,24,2048]{2,1,0:T(8,128)(2,1)}, u32[]{:S(2)}, u32[]{:S(2)}) async-start(bf16[4,24,2048]{2,1,0:T(8,128)(2,1)} %get-tuple-element.58), calls=%async_computation.4 | async-start | bytes 786432 | tf_op jit(solution)/shard_map/all_to_all | solution.py:41
  223.6 1.8 collective-permute-start.18
  226.2 21.4 %copy-start.69 = (s32[24,1]{0,1:T(1,128)S(1)}, s32[24,1]{0,1:T(1,128)}, u32[]{:S(2)}) copy-start(s32[24,1]{0,1:T(1,128)} %get-tuple-element.91) | copy-start | bytes 292
  226.2 18.1 %all-to-all-start.9 = ((bf16[4,24,2048]{2,1,0:T(8,128)(2,1)}), bf16[4,24,2048]{2,1,0:T(8,128)(2,1)S(1)}, u32[]{:S(2)}, u32[]{:S(2)}) async-start(bf16[4,24,2048]{2,1,0:T(8,128)(2,1)} %copy-done.5), calls=%async_computation.9 | async-start | bytes 786432 | tf_op jit(solution)/shard_map/all_to_all | solution.py:41
  231.3 31.1 %copy-start.46 = (s32[1,24]{1,0:T(1,128)S(1)}, s32[1,24]{1,0:T(1,128)}, u32[]{:S(2)}) copy-start(s32[1,24]{1,0:T(1,128)} %get-tuple-element.100.row.ahead_row) | copy-start | bytes 292
  233.5 26.8 %collective-permute-start.16 = (bf16[64,4096]{1,0:T(8,128)(2,1)S(1)}, bf16[64,4096]{1,0:T(8,128)(2,1)}, u32[]{:S(2)}, u32[]{:S(2)}) collective-permute-start(bf16[64,4096]{1,0:T(8,128)(2,1)S(1)} %shard_map.145.act), channel_id=1, source_target_pairs={{8,0},{16,8},{24,16},{9,1},{17,9},{25,17},{10,2},{18,10},{26,18},{... | collective-permute-start | bytes 1572872 | tf_op jit(solution)/shard_map/ppermute | solution.py:25
  244.2 24.9 %collective-permute-start.9 = (bf16[4,24,2048]{2,1,0:T(8,128)(2,1)}, bf16[4,24,2048]{2,1,0:T(8,128)(2,1)}, u32[]{:S(2)}, u32[]{:S(2)}) collective-permute-start(bf16[4,24,2048]{2,1,0:T(8,128)(2,1)} %all-to-all-done.4.near), channel_id=1, source_target_pairs={{0,1},{1,0},{2,3},{3,2},{4,5},{5,4},{6,7},{7,6},{8,9},{9,8},{10,11... | collective-permute-start | bytes 1179656 | tf_op jit(solution)/shard_map/ppermute | solution.py:30
  246.3 16.1 %collective-permute-start.19 = (bf16[24,2048]{1,0:T(8,128)(2,1)}, bf16[24,2048]{1,0:T(8,128)(2,1)S(1)}, u32[]{:S(2)}, u32[]{:S(2)}) collective-permute-start(bf16[24,2048]{1,0:T(8,128)(2,1)} %shard_map.150.rows), channel_id=1, source_target_pairs={{8,0},{16,8},{24,16},{9,1},{17,9},{25,17},{10,2},{18,10},{26,18},{... | collective-permute-start | bytes 294920 | tf_op jit(solution)/shard_map/ppermute | solution.py:25
  264.0 17.8 %all-to-all-start.10 = ((bf16[4,24,2048]{2,1,0:T(8,128)(2,1)}), bf16[4,24,2048]{2,1,0:T(8,128)(2,1)}, u32[]{:S(2)}, u32[]{:S(2)}) async-start(bf16[4,24,2048]{2,1,0:T(8,128)(2,1)} %get-tuple-element.76), calls=%async_computation.10 | async-start | bytes 786432 | tf_op jit(solution)/shard_map/all_to_all | solution.py:41
  281.9 2.1 collective-permute-start.10
  281.9 9.0 %collective-permute-start.20 = (bf16[4,24,2048]{2,1,0:T(8,128)(2,1)}, bf16[4,24,2048]{2,1,0:T(8,128)(2,1)}, u32[]{:S(2)}, u32[]{:S(2)}) collective-permute-start(bf16[4,24,2048]{2,1,0:T(8,128)(2,1)} %all-to-all-done.10.near_g), channel_id=1, source_target_pairs={{0,1},{1,0},{2,3},{3,2},{4,5},{5,4},{6,7},{7,6},{8,9},{9,8},{10,11... | collective-permute-start | bytes 1179656 | tf_op jit(solution)/shard_map/ppermute | solution.py:30
  285.7 30.6 %all-to-all-start.5 = ((bf16[4,24,2048]{2,1,0:T(8,128)(2,1)}), bf16[4,24,2048]{2,1,0:T(8,128)(2,1)S(1)}, u32[]{:S(2)}, u32[]{:S(2)}) async-start(bf16[4,24,2048]{2,1,0:T(8,128)(2,1)} %shard_map.135), calls=%async_computation.5 | async-start | bytes 786432 | tf_op jit(solution)/shard_map/all_to_all | solution.py:41
  307.7 7.7 %collective-permute-start.21 = (bf16[4,24,2048]{2,1,0:T(8,128)(2,1)S(1)}, bf16[4,24,2048]{2,1,0:T(8,128)(2,1)S(1)}, u32[]{:S(2)}, u32[]{:S(2)}) collective-permute-start(bf16[4,24,2048]{2,1,0:T(8,128)(2,1)S(1)} %get-tuple-element.79), channel_id=1, source_target_pairs={{0,1},{1,0},{2,3},{3,2},{4,5},{5,4},{6,7},{7,6},{8,9},{9,8},{10,11... | collective-permute-start | bytes 1179656 | tf_op jit(solution)/shard_map/ppermute | solution.py:30
  307.8 1.7 collective-permute-start.22
  309.6 19.8 %collective-permute-start.23 = (f32[2,2048]{1,0:T(2,128)S(1)}, f32[2,2048]{1,0:T(2,128)S(1)}, u32[]{:S(2)}, u32[]{:S(2)}) collective-permute-start(f32[2,2048]{1,0:T(2,128)S(1)} %add.69), channel_id=1, source_target_pairs={{0,2},{1,3},{2,4},{3,5},{4,6},{5,7},{6,0},{7,1},{8,10},{9,11},{10,... | collective-permute-start | bytes 49160 | tf_op jit(solution)/shard_map/ppermute | solution.py:35
  311.7 17.7 %collective-permute-start.24 = (f32[2,2048]{1,0:T(2,128)S(1)}, f32[2,2048]{1,0:T(2,128)}, u32[]{:S(2)}, u32[]{:S(2)}) collective-permute-start(f32[2,2048]{1,0:T(2,128)S(1)} %add.69), channel_id=1, source_target_pairs={{0,4},{1,5},{2,6},{3,7},{4,0},{5,1},{6,2},{7,3},{8,12},{9,13},{10,... | collective-permute-start | bytes 49160 | tf_op jit(solution)/shard_map/ppermute | solution.py:35
  314.0 15.4 %collective-permute-start.25 = (f32[2,2048]{1,0:T(2,128)S(1)}, f32[2,2048]{1,0:T(2,128)}, u32[]{:S(2)}, u32[]{:S(2)}) collective-permute-start(f32[2,2048]{1,0:T(2,128)S(1)} %add.69), channel_id=1, source_target_pairs={{0,6},{1,7},{2,0},{3,1},{4,2},{5,3},{6,4},{7,5},{8,14},{9,15},{10,... | collective-permute-start | bytes 49160 | tf_op jit(solution)/shard_map/ppermute | solution.py:35
  316.3 14.9 %all-to-all-start.11 = ((bf16[4,24,2048]{2,1,0:T(8,128)(2,1)}), bf16[4,24,2048]{2,1,0:T(8,128)(2,1)S(1)}, u32[]{:S(2)}, u32[]{:S(2)}) async-start(bf16[4,24,2048]{2,1,0:T(8,128)(2,1)} %copy-done.4), calls=%async_computation.11 | async-start | bytes 786432 | tf_op jit(solution)/shard_map/all_to_all | solution.py:41
  (61 other events, 221.5 us)
